TPU v7x, 256 devices: a whole 4x4x8 slice. The times are simulated.
256 devices in a mesh: pack: 32 (over y, x, core), dp: 8 (over z).
Axes of the slice: x: 4, y: 4, z: 8, core: 2. Of those that a mesh axis runs over, the one named last changes fastest.
Arguments:
- queries: bfloat16 [65536, 1024], P(('dp', 'pack')), parts along dimension 0, may hold values from -16 to 16
- keys: bfloat16 [65536, 1024], P(('dp', 'pack')), parts along dimension 0, may hold values from -16 to 16
- values: bfloat16 [65536, 1024], P(('dp', 'pack')), parts along dimension 0, may hold values from -24 to 24
- residual: bfloat16 [65536, 1024], P(('dp', 'pack')), parts along dimension 0, may hold values from -6 to 6
- segments: int32 [65536], P(('dp', 'pack')), parts along dimension 0, may hold values from 0 to 31, never falling along the last dimension, each value on 1 to 512 neighbouring positions
- out_weight: bfloat16 [1024, 1024], replicated, may hold values from -0.1875 to 0.1875
- norm_gain: float32 [1024], replicated, may hold values from 0.25 to 1.75
- routes: int32 [65536, 1], P(('dp', 'pack')), parts along dimension 0, may hold values from 0 to 31; in each aligned block of 256 rows (0 to 255, 256 to 511, ...) at most 16 rows name the same one
- gate_prob: float32 [65536], P(('dp', 'pack')), parts along dimension 0, may hold values from 0.2 to 1
- expert_in: bfloat16 [32, 1024, 2048], P('pack'), may hold values from -0.1875 to 0.1875
- expert_out: bfloat16 [32, 2048, 1024], P('pack'), may hold values from -0.125 to 0.125
Outputs:
- layer_out: bfloat16 [65536, 1024], P(('dp', 'pack')), parts along dimension 0
There are 8 independent parts, one for each index of `dp`. A program takes and returns all parts, laid end to end along the dimension named above; an argument that names none is the same for every part. Nothing has to cross between parts.
Inputs may be any that keep to these rules, and one draw needn't show every extreme that they name: `segments`: segment numbers never fall along the pack; each image covers 1 to 512 patches, one exactly 512. `routes`: among one device's 256 patches no expert is named more than 16 times; some device names some expert exactly 16 times.
All inputs are finite; a program needn't handle non-finite values.
Results may differ from a plain program's by a relative error of at most 0.0051.
Values may be sent and summed in bfloat16 or wider, within the bound.
A program may use at most 128 MiB of HBM per device.

v0:
```python
from functools import reduce

import jax
import jax.numpy as jnp
from jax import lax
from jax.sharding import PartitionSpec as P

HEADS = 16
MAXLEN = 512


NEGATIVE = -1e30


def from_behind(value, axis, by):
    peers = lax.axis_size(axis)
    pairs = [(i, i + by) for i in range(peers) if 0 <= i + by < peers]
    return lax.ppermute(value, axis, pairs)


def tile_scores(query_part, key_part, key_marks, own_marks, score_scale):
    scores = (
        jnp.einsum("qhd,khd->hqk", query_part, key_part, preferred_element_type=jnp.float32)
        * score_scale
    )
    same_image = own_marks[:, None] == key_marks[None, :]
    return jnp.where(same_image[None, :, :], scores, NEGATIVE)


def tile_values(exp_scores, value_part):
    return jnp.einsum(
        "hqk,khd->qhd",
        exp_scores.astype(jnp.bfloat16),
        value_part,
        preferred_element_type=jnp.float32,
    )


def on_device(
    queries,
    keys,
    values,
    residual,
    segments,
    out_weight,
    norm_gain,
    routes,
    gate_prob,
    expert_in,
    expert_out,
):
    row_count, width_all = queries.shape
    head_count = HEADS
    head_width = width_all // head_count
    reach_count = (MAXLEN + row_count - 2) // row_count
    score_scale = head_width ** (-0.5)
    own_marks = segments + 1
    lower_tiles = []
    upper_tiles = []
    for offset in range(1, reach_count + 1):
        lower_tiles.append(from_behind((keys, values, own_marks), "pack", offset))
        upper_tiles.append(from_behind((keys, values, own_marks), "pack", -offset))
    tile_list = lower_tiles[::-1] + [(keys, values, own_marks)] + upper_tiles
    query_heads = queries.reshape(row_count, head_count, head_width)
    key_heads = [entry[0].reshape(row_count, head_count, head_width) for entry in tile_list]
    value_heads = [entry[1].reshape(row_count, head_count, head_width) for entry in tile_list]
    pieces = []
    for head_start in range(0, head_count, 4):
        query_part = query_heads[:, head_start : head_start + 4]
        score_list = []
        for number in range(len(tile_list)):
            key_part = key_heads[number][:, head_start : head_start + 4]
            scores = tile_scores(query_part, key_part, tile_list[number][2], own_marks, score_scale)
            score_list.append(scores)
        row_top = reduce(jnp.maximum, [scores.max(axis=2) for scores in score_list])
        row_total = jnp.zeros_like(row_top)
        summed = jnp.zeros((row_count, 4, head_width), jnp.float32)
        for number in range(len(score_list)):
            exp_scores = jnp.exp(score_list[number] - row_top[:, :, None])
            row_total = row_total + exp_scores.sum(axis=2)
            value_part = value_heads[number][:, head_start : head_start + 4]
            contrib = tile_values(exp_scores, value_part)
            summed = summed + contrib
        pieces.append(summed / row_total.T[:, :, None])
    attended = jnp.concatenate(pieces, axis=1).reshape(row_count, width_all).astype(jnp.bfloat16)
    stream = residual.astype(jnp.float32) + jnp.dot(
        attended, out_weight, preferred_element_type=jnp.float32
    )
    feature_mean = jnp.mean(stream, axis=1, keepdims=True)
    centered = stream - feature_mean
    feature_var = jnp.mean(centered * centered, axis=1, keepdims=True)
    normed = (centered * lax.rsqrt(feature_var + 1e-06) * norm_gain).astype(jnp.bfloat16)
    local_experts = expert_in.shape[0]
    device_count = lax.axis_size("pack")
    expert_total = local_experts * device_count
    capacity = 2 * row_count // device_count
    expert_ids = routes[:, 0]
    onehot = (expert_ids[:, None] == jnp.arange(expert_total, dtype=jnp.int32)[None, :]).astype(
        jnp.int32
    )
    rank_table = jnp.cumsum(onehot, axis=0) - onehot
    slot_of = jnp.sum(rank_table * onehot, axis=1)
    target = expert_ids * capacity + slot_of
    place_table = (
        target[None, :] == jnp.arange(expert_total * capacity, dtype=jnp.int32)[:, None]
    ).astype(jnp.bfloat16)
    outgoing = jnp.dot(place_table, normed, preferred_element_type=jnp.float32).astype(jnp.bfloat16)
    outgoing = outgoing.reshape(expert_total, capacity, width_all)
    received = lax.all_to_all(outgoing, "pack", split_axis=0, concat_axis=0, tiled=True)
    sources = received.shape[0] // local_experts
    slot_count = received.shape[1]
    grouped = received.reshape(sources, local_experts, slot_count, width_all)
    hidden = jnp.einsum("sepd,edf->sepf", grouped, expert_in, preferred_element_type=jnp.float32)
    hidden = jax.nn.gelu(hidden, approximate=False).astype(jnp.bfloat16)
    produced = jnp.einsum(
        "sepf,efd->sepd", hidden, expert_out, preferred_element_type=jnp.float32
    ).astype(jnp.bfloat16)
    produced = produced.reshape(sources * local_experts, slot_count, width_all)
    returned = lax.all_to_all(produced, "pack", split_axis=0, concat_axis=0, tiled=True)
    expert_result = jnp.dot(
        place_table.T,
        returned.reshape(expert_total * capacity, width_all),
        preferred_element_type=jnp.float32,
    )
    layer_out = stream + gate_prob[:, None] * expert_result
    return layer_out.astype(jnp.bfloat16)


def solution(mesh):
    placed = (
        P(("dp", "pack"), None),
        P(("dp", "pack"), None),
        P(("dp", "pack"), None),
        P(("dp", "pack"), None),
        P(("dp", "pack")),
        P(),
        P(),
        P(("dp", "pack"), None),
        P(("dp", "pack")),
        P("pack", None, None),
        P("pack", None, None),
    )
    return jax.shard_map(
        on_device, mesh=mesh, in_specs=placed, out_specs=P(("dp", "pack"), None), check_vma=False
    )
```

profile of v0, /device:TPU:1, one launch (start us, length us, event | category | flops | bytes accessed | tf_op | source)
XLA Modules:
  0.0 206.1 jit_solution(5765820314506032544)
XLA Ops:
  0.8 3.9 %collective-permute-start = (s32[256]{0:T(256)S(1)}, s32[256]{0:T(256)S(1)}, u32[]{:S(2)}, u32[]{:S(2)}) collective-permute-start(s32[256]{0:T(256)S(1)} %broadcast_add_fusion), channel_id=1, source_target_pairs={{0,16},{8,24},{16,32},{24,40},{32,48},{40,56},{48,64},{56,72},{64,... | collective-permute-start | bytes 3080 | tf_op jit(solution)/shard_map/ppermute | solution.py:18
  4.8 4.0 %collective-permute-start.2 = (s32[256]{0:T(256)S(1)}, s32[256]{0:T(256)S(1)}, u32[]{:S(2)}, u32[]{:S(2)}) collective-permute-start(s32[256]{0:T(256)S(1)} %broadcast_add_fusion), channel_id=1, source_target_pairs={{0,8},{8,16},{16,24},{24,32},{32,40},{40,48},{48,56},{56,64},{64,7... | collective-permute-start | bytes 3080 | tf_op jit(solution)/shard_map/ppermute | solution.py:18
  23.7 5.8 %collective-permute-start.1 = (bf16[256,1024]{1,0:T(8,128)(2,1)}, bf16[256,1024]{1,0:T(8,128)(2,1)}, u32[]{:S(2)}, u32[]{:S(2)}) collective-permute-start(bf16[256,1024]{1,0:T(8,128)(2,1)} %param.12), channel_id=1, source_target_pairs={{0,16},{8,24},{16,32},{24,40},{32,48},{40,56},{48,64},{56,72},{64,... | collective-permute-start | bytes 1572872 | tf_op jit(solution)/shard_map/ppermute | solution.py:18
  29.5 3.0 %collective-permute-start.3 = (bf16[256,1024]{1,0:T(8,128)(2,1)}, bf16[256,1024]{1,0:T(8,128)(2,1)}, u32[]{:S(2)}, u32[]{:S(2)}) collective-permute-start(bf16[256,1024]{1,0:T(8,128)(2,1)} %param.12), channel_id=1, source_target_pairs={{0,8},{8,16},{16,24},{24,32},{32,40},{40,48},{48,56},{56,64},{64,7... | collective-permute-start | bytes 1572872 | tf_op jit(solution)/shard_map/ppermute | solution.py:18
  37.2 2.3 %fusion.285 = (f32[4,256]{1,0:T(4,128)S(1)}, f32[4,256,256]{1,2,0:T(8,128)}) fusion(bf16[256,16,64]{0,2,1:T(8,128)(2,1)S(1)} %bitcast.205, bf16[256,16,64]{0,2,1:T(8,128)(2,1)} %bitcast.229, pred[256,256]{0,1:T(8,128)(4,1)S(1)} %get-tuple-element.26), kind=kOutput, calls=%fused_computation.337 | convolution fusion | flops 34339840 | bytes 1773568 | tf_op jit(solution)/shard_map/qhd,khd->hqk/dot_general | solution.py:23
  44.8 4.5 %collective-permute-start.8 = (bf16[256,1024]{1,0:T(8,128)(2,1)}, bf16[256,1024]{1,0:T(8,128)(2,1)}, u32[]{:S(2)}, u32[]{:S(2)}) collective-permute-start(bf16[256,1024]{1,0:T(8,128)(2,1)} %param.13), channel_id=1, source_target_pairs={{0,16},{8,24},{16,32},{24,40},{32,48},{40,56},{48,64},{56,72},{64,... | collective-permute-start | bytes 1572872 | tf_op jit(solution)/shard_map/ppermute | solution.py:18
  56.5 2.3 %fusion.289 = (f32[4,256]{1,0:T(4,128)S(1)}, f32[4,256,256]{1,2,0:T(8,128)}) fusion(bf16[256,16,64]{0,2,1:T(8,128)(2,1)S(1)} %bitcast.210, bf16[256,16,64]{0,2,1:T(8,128)(2,1)} %bitcast.232, pred[256,256]{0,1:T(8,128)(4,1)S(1)} %get-tuple-element.27), kind=kOutput, calls=%fused_computation.341 | convolution fusion | flops 34339840 | bytes 1773568 | tf_op jit(solution)/shard_map/qhd,khd->hqk/dot_general | solution.py:23
  60.1 2.6 %collective-permute-start.10 = (bf16[256,1024]{1,0:T(8,128)(2,1)}, bf16[256,1024]{1,0:T(8,128)(2,1)}, u32[]{:S(2)}, u32[]{:S(2)}) collective-permute-start(bf16[256,1024]{1,0:T(8,128)(2,1)} %param.13), channel_id=1, source_target_pairs={{8,0},{16,8},{24,16},{32,24},{40,32},{48,40},{56,48},{64,56},{72,6... | collective-permute-start | bytes 1572872 | tf_op jit(solution)/shard_map/ppermute | solution.py:18
  64.9 2.4 %fusion.291 = (f32[4,256]{1,0:T(4,128)S(1)}, f32[4,256,256]{1,2,0:T(8,128)}) fusion(bf16[256,16,64]{0,2,1:T(8,128)(2,1)} %bitcast.212, bf16[256,16,64]{0,2,1:T(8,128)(2,1)} %bitcast.236, pred[256,256]{0,1:T(8,128)(4,1)S(1)} %get-tuple-element.29), kind=kOutput, calls=%fused_computation.343 | convolution fusion | flops 34339840 | bytes 1773568 | tf_op jit(solution)/shard_map/qhd,khd->hqk/dot_general | solution.py:23
  67.2 2.4 %fusion.286 = (f32[4,256]{1,0:T(4,128)S(1)}, f32[4,256,256]{1,2,0:T(8,128)}) fusion(bf16[256,16,64]{0,2,1:T(8,128)(2,1)} %bitcast.213, bf16[256,16,64]{0,2,1:T(8,128)(2,1)} %bitcast.237, pred[256,256]{0,1:T(8,128)(4,1)S(1)} %get-tuple-element.29), kind=kOutput, calls=%fused_computation.338 | convolution fusion | flops 34339840 | bytes 1773568 | tf_op jit(solution)/shard_map/qhd,khd->hqk/dot_general | solution.py:23
  71.7 2.5 %fusion.292 = (f32[4,256]{1,0:T(4,128)S(1)}, f32[4,256,256]{1,2,0:T(8,128)}) fusion(bf16[256,16,64]{0,2,1:T(8,128)(2,1)} %bitcast.214, bf16[256,16,64]{0,2,1:T(8,128)(2,1)} %bitcast.240, pred[256,256]{0,1:T(8,128)(4,1)S(1)} %get-tuple-element.25), kind=kOutput, calls=%fused_computation.344 | convolution fusion | flops 34339840 | bytes 1773568 | tf_op jit(solution)/shard_map/qhd,khd->hqk/dot_general | solution.py:23
  74.1 2.4 %fusion.287 = (f32[4,256]{1,0:T(4,128)S(1)}, f32[4,256,256]{1,2,0:T(8,128)}) fusion(bf16[256,16,64]{0,2,1:T(8,128)(2,1)} %bitcast.215, bf16[256,16,64]{0,2,1:T(8,128)(2,1)} %bitcast.241, pred[256,256]{0,1:T(8,128)(4,1)S(1)} %get-tuple-element.25), kind=kOutput, calls=%fused_computation.339 | convolution fusion | flops 34339840 | bytes 1773568 | tf_op jit(solution)/shard_map/qhd,khd->hqk/dot_general | solution.py:23
  76.5 2.3 %fusion.278 = (f32[4,256]{1,0:T(4,128)S(1)}, f32[4,256,256]{1,2,0:T(8,128)}) fusion(bf16[256,16,64]{0,2,1:T(8,128)(2,1)} %bitcast.216, bf16[256,16,64]{0,2,1:T(8,128)(2,1)} %bitcast.226, pred[256,256]{0,1:T(8,128)(4,1)S(1)} %get-tuple-element.28), kind=kOutput, calls=%fused_computation.330 | convolution fusion | flops 34339840 | bytes 1773568 | tf_op jit(solution)/shard_map/qhd,khd->hqk/dot_general | solution.py:23
  90.6 2.3 %fusion.169 = f32[4,256,64]{1,2,0:T(8,128)} fusion(f32[4,256,256]{1,2,0:T(8,128)} %get-tuple-element.65, f32[4,256]{1,0:T(4,128)S(1)} %maximum_maximum_fusion.3, bf16[256,16,64]{0,2,1:T(8,128)(2,1)} %bitcast.188), kind=kOutput, calls=%fused_computation.200 | convolution fusion | flops 34078720 | bytes 1445888 | tf_op jit(solution)/shard_map/hqk,khd->qhd/dot_general | solution.py:31
  92.9 2.3 %fusion.163 = f32[4,256,64]{1,2,0:T(8,128)} fusion(f32[4,256,256]{1,2,0:T(8,128)} %get-tuple-element.59, f32[4,256]{1,0:T(4,128)S(1)} %maximum_maximum_fusion.2, bf16[256,16,64]{0,2,1:T(8,128)(2,1)} %bitcast.193), kind=kOutput, calls=%fused_computation.198 | convolution fusion | flops 34078720 | bytes 1445888 | tf_op jit(solution)/shard_map/hqk,khd->qhd/dot_general | solution.py:31
  101.4 2.5 %fusion.166 = f32[4,256,64]{1,2,0:T(8,128)} fusion(f32[4,256,256]{1,2,0:T(8,128)} %get-tuple-element.61, f32[4,256]{1,0:T(4,128)S(1)} %maximum_maximum_fusion.3, bf16[256,16,64]{0,2,1:T(8,128)(2,1)} %bitcast.196), kind=kOutput, calls=%fused_computation.199 | convolution fusion | flops 34078720 | bytes 1445888 | tf_op jit(solution)/shard_map/hqk,khd->qhd/dot_general | solution.py:31
  103.9 2.4 %fusion.158 = f32[4,256,64]{1,2,0:T(8,128)} fusion(f32[4,256,256]{1,2,0:T(8,128)} %get-tuple-element.51, f32[4,256]{1,0:T(4,128)S(1)} %maximum_maximum_fusion.2, bf16[256,16,64]{0,2,1:T(8,128)(2,1)} %bitcast.197), kind=kOutput, calls=%fused_computation.196 | convolution fusion | flops 34078720 | bytes 1445888 | tf_op jit(solution)/shard_map/hqk,khd->qhd/dot_general | solution.py:31
  106.4 2.3 %fusion.155 = f32[4,256,64]{1,2,0:T(8,128)} fusion(f32[4,256,256]{1,2,0:T(8,128)} %get-tuple-element.49, f32[4,256]{1,0:T(4,128)S(1)} %maximum_maximum_fusion.1, bf16[256,16,64]{0,2,1:T(8,128)(2,1)} %bitcast.194), kind=kOutput, calls=%fused_computation.195 | convolution fusion | flops 34078720 | bytes 1445888 | tf_op jit(solution)/shard_map/hqk,khd->qhd/dot_general | solution.py:31
  120.2 2.5 %fusion.82 = f32[4,256,64]{1,2,0:T(8,128)} fusion(f32[4,256,64]{1,2,0:T(8,128)} %fusion.169, f32[4,256,64]{1,2,0:T(8,128)S(1)} %fusion.171, f32[4,256,256]{1,2,0:T(8,128)} %get-tuple-element.67, f32[4,256]{1,0:T(4,128)S(1)} %maximum_maximum_fusion.3, bf16[256,16,64]{0,2,1:T(8,128)(2,1)} %bitcast.200), kind=kOutput, calls=%fused_computation.108 | convolution fusion | flops 34209792 | bytes 1970176 | tf_op jit(solution)/shard_map/hqk,khd->qhd/dot_general | solution.py:31
  122.7 2.5 %fusion.85 = f32[4,256,64]{1,2,0:T(8,128)} fusion(f32[4,256,64]{1,2,0:T(8,128)} %fusion.161, f32[4,256,64]{1,2,0:T(8,128)} %fusion.163, f32[4,256,256]{1,2,0:T(8,128)} %get-tuple-element.57, f32[4,256]{1,0:T(4,128)S(1)} %maximum_maximum_fusion.2, bf16[256,16,64]{0,2,1:T(8,128)(2,1)} %bitcast.201), kind=kOutput, calls=%fused_computation.111 | convolution fusion | flops 34209792 | bytes 1970176 | tf_op jit(solution)/shard_map/hqk,khd->qhd/dot_general | solution.py:31
  125.2 2.5 %fusion.124 = (f32[4,256]{1,0:T(4,128)S(1)}, f32[4,256]{1,0:T(4,128)S(1)}, f32[4,256]{1,0:T(4,128)S(1)}, f32[4,256]{1,0:T(4,128)S(1)}, f32[4,256]{1,0:T(4,128)S(1)}) fusion(f32[4,256,256]{1,2,0:T(8,128)} %get-tuple-element.49, f32[4,256]{1,0:T(4,128)S(1)} %maximum_maximum_fusion.1, f32[4,256,256]{1,2,0:T(8,128)} %get-tuple-element.47, ...), kind=kLoop, calls=%fused_computation.172 | loop fusion | flops 2616320 | bytes 5267456 | tf_op jit(solution)/shard_map/reduce_sum | solution.py:80
  139.9 27.0 %all_to_all.10 = bf16[32,16,1024]{2,1,0:T(8,128)(2,1)} all-to-all(bf16[32,16,1024]{2,1,0:T(8,128)(2,1)S(1)} %bitcast.182), channel_id=1, replica_groups=mesh['pack'=32,'dp'=8] {'pack'}, dimensions={0} | all-to-all | bytes 2097152 | tf_op jit(solution)/shard_map/all_to_all | solution.py:109
  166.9 16.7 %fusion.53 = bf16[32,16,1024]{2,1,0:T(8,128)(2,1)} fusion(bf16[1,2048,1024]{2,1,0:T(8,128)(2,1)} %param.21, bf16[32,16,1024]{2,1,0:T(8,128)(2,1)} %all_to_all.10, bf16[1,1024,2048]{2,1,0:T(8,128)(2,1)} %param.20), kind=kOutput, calls=%fused_computation.55 | convolution fusion | flops 4363649024 | bytes 10485760 | tf_op jit(solution)/shard_map/sepf,efd->sepd/dot_general | solution.py:115
  183.6 21.3 %all_to_all.11 = bf16[32,16,1024]{2,1,0:T(8,128)(2,1)S(1)} all-to-all(bf16[32,16,1024]{2,1,0:T(8,128)(2,1)} %fusion.53), channel_id=1, replica_groups=mesh['pack'=32,'dp'=8] {'pack'}, dimensions={0} | all-to-all | bytes 2097152 | tf_op jit(solution)/shard_map/all_to_all | solution.py:119
  (170 shorter events, 81.1 us)
Async XLA Ops:
  0.0 138.2 %copy-start = (bf16[1024,1024]{1,0:T(8,128)(2,1)S(1)}, bf16[1024,1024]{1,0:T(8,128)(2,1)}, u32[]{:S(2)}) copy-start(bf16[1024,1024]{1,0:T(8,128)(2,1)} %param.16) | copy-start | bytes 6291460
  0.8 20.9 %collective-permute-start = (s32[256]{0:T(256)S(1)}, s32[256]{0:T(256)S(1)}, u32[]{:S(2)}, u32[]{:S(2)}) collective-permute-start(s32[256]{0:T(256)S(1)} %broadcast_add_fusion), channel_id=1, source_target_pairs={{0,16},{8,24},{16,32},{24,40},{32,48},{40,56},{48,64},{56,72},{64,... | collective-permute-start | bytes 3080 | tf_op jit(solution)/shard_map/ppermute | solution.py:18
  4.8 18.9 %collective-permute-start.2 = (s32[256]{0:T(256)S(1)}, s32[256]{0:T(256)S(1)}, u32[]{:S(2)}, u32[]{:S(2)}) collective-permute-start(s32[256]{0:T(256)S(1)} %broadcast_add_fusion), channel_id=1, source_target_pairs={{0,8},{8,16},{16,24},{24,32},{32,40},{40,48},{48,56},{56,64},{64,7... | collective-permute-start | bytes 3080 | tf_op jit(solution)/shard_map/ppermute | solution.py:18
  8.7 20.8 %collective-permute-start.4 = (s32[256]{0:T(256)S(1)}, s32[256]{0:T(256)S(1)}, u32[]{:S(2)}, u32[]{:S(2)}) collective-permute-start(s32[256]{0:T(256)S(1)} %broadcast_add_fusion), channel_id=1, source_target_pairs={{8,0},{16,8},{24,16},{32,24},{40,32},{48,40},{56,48},{64,56},{72,6... | collective-permute-start | bytes 3080 | tf_op jit(solution)/shard_map/ppermute | solution.py:18
  10.7 21.9 %collective-permute-start.6 = (s32[256]{0:T(256)S(1)}, s32[256]{0:T(256)S(1)}, u32[]{:S(2)}, u32[]{:S(2)}) collective-permute-start(s32[256]{0:T(256)S(1)} %broadcast_add_fusion), channel_id=1, source_target_pairs={{16,0},{24,8},{32,16},{40,24},{48,32},{56,40},{64,48},{72,56},{80,... | collective-permute-start | bytes 3080 | tf_op jit(solution)/shard_map/ppermute | solution.py:18
  12.0 32.0 %collective-permute-start.7 = (bf16[256,1024]{1,0:T(8,128)(2,1)}, bf16[256,1024]{1,0:T(8,128)(2,1)S(1)}, u32[]{:S(2)}, u32[]{:S(2)}) collective-permute-start(bf16[256,1024]{1,0:T(8,128)(2,1)} %param.12), channel_id=1, source_target_pairs={{16,0},{24,8},{32,16},{40,24},{48,32},{56,40},{64,48},{72,56},{80,... | collective-permute-start | bytes 1572872 | tf_op jit(solution)/shard_map/ppermute | solution.py:18
  19.5 37.0 %copy-start.34 = (bf16[256,1024]{0,1:T(8,128)(2,1)}, bf16[256,1024]{0,1:T(8,128)(2,1)S(1)}, u32[]{:S(2)}) copy-start(bf16[256,1024]{0,1:T(8,128)(2,1)S(1)} %copy.43) | copy-start | bytes 1572868
  21.8 31.4 %collective-permute-start.5 = (bf16[256,1024]{1,0:T(8,128)(2,1)}, bf16[256,1024]{1,0:T(8,128)(2,1)}, u32[]{:S(2)}, u32[]{:S(2)}) collective-permute-start(bf16[256,1024]{1,0:T(8,128)(2,1)} %param.12), channel_id=1, source_target_pairs={{8,0},{16,8},{24,16},{32,24},{40,32},{48,40},{56,48},{64,56},{72,6... | collective-permute-start | bytes 1572872 | tf_op jit(solution)/shard_map/ppermute | solution.py:18
  23.7 36.4 %collective-permute-start.1 = (bf16[256,1024]{1,0:T(8,128)(2,1)}, bf16[256,1024]{1,0:T(8,128)(2,1)}, u32[]{:S(2)}, u32[]{:S(2)}) collective-permute-start(bf16[256,1024]{1,0:T(8,128)(2,1)} %param.12), channel_id=1, source_target_pairs={{0,16},{8,24},{16,32},{24,40},{32,48},{40,56},{48,64},{56,72},{64,... | collective-permute-start | bytes 1572872 | tf_op jit(solution)/shard_map/ppermute | solution.py:18
  29.5 40.1 %collective-permute-start.3 = (bf16[256,1024]{1,0:T(8,128)(2,1)}, bf16[256,1024]{1,0:T(8,128)(2,1)}, u32[]{:S(2)}, u32[]{:S(2)}) collective-permute-start(bf16[256,1024]{1,0:T(8,128)(2,1)} %param.12), channel_id=1, source_target_pairs={{0,8},{8,16},{16,24},{24,32},{32,40},{40,48},{48,56},{56,64},{64,7... | collective-permute-start | bytes 1572872 | tf_op jit(solution)/shard_map/ppermute | solution.py:18
  32.6 54.2 %collective-permute-start.9 = (bf16[256,1024]{1,0:T(8,128)(2,1)}, bf16[256,1024]{1,0:T(8,128)(2,1)}, u32[]{:S(2)}, u32[]{:S(2)}) collective-permute-start(bf16[256,1024]{1,0:T(8,128)(2,1)} %param.13), channel_id=1, source_target_pairs={{0,8},{8,16},{16,24},{24,32},{32,40},{40,48},{48,56},{56,64},{64,7... | collective-permute-start | bytes 1572872 | tf_op jit(solution)/shard_map/ppermute | solution.py:18
  44.8 73.3 %collective-permute-start.8 = (bf16[256,1024]{1,0:T(8,128)(2,1)}, bf16[256,1024]{1,0:T(8,128)(2,1)}, u32[]{:S(2)}, u32[]{:S(2)}) collective-permute-start(bf16[256,1024]{1,0:T(8,128)(2,1)} %param.13), channel_id=1, source_target_pairs={{0,16},{8,24},{16,32},{24,40},{32,48},{40,56},{48,64},{56,72},{64,... | collective-permute-start | bytes 1572872 | tf_op jit(solution)/shard_map/ppermute | solution.py:18
  53.2 46.2 %collective-permute-start.11 = (bf16[256,1024]{1,0:T(8,128)(2,1)}, bf16[256,1024]{1,0:T(8,128)(2,1)}, u32[]{:S(2)}, u32[]{:S(2)}) collective-permute-start(bf16[256,1024]{1,0:T(8,128)(2,1)} %param.13), channel_id=1, source_target_pairs={{16,0},{24,8},{32,16},{40,24},{48,32},{56,40},{64,48},{72,56},{80,... | collective-permute-start | bytes 1572872 | tf_op jit(solution)/shard_map/ppermute | solution.py:18
  60.1 69.7 %collective-permute-start.10 = (bf16[256,1024]{1,0:T(8,128)(2,1)}, bf16[256,1024]{1,0:T(8,128)(2,1)}, u32[]{:S(2)}, u32[]{:S(2)}) collective-permute-start(bf16[256,1024]{1,0:T(8,128)(2,1)} %param.13), channel_id=1, source_target_pairs={{8,0},{16,8},{24,16},{32,24},{40,32},{48,40},{56,48},{64,56},{72,6... | collective-permute-start | bytes 1572872 | tf_op jit(solution)/shard_map/ppermute | solution.py:18
  71.7 8.5 %copy-start.40 = (bf16[256,1024]{0,1:T(8,128)(2,1)S(1)}, bf16[256,1024]{0,1:T(8,128)(2,1)}, u32[]{:S(2)}) copy-start(bf16[256,1024]{0,1:T(8,128)(2,1)} %copy.44) | copy-start | bytes 1572868
  71.7 9.8 %copy-start.41 = (bf16[256,1024]{0,1:T(8,128)(2,1)S(1)}, bf16[256,1024]{0,1:T(8,128)(2,1)}, u32[]{:S(2)}) copy-start(bf16[256,1024]{0,1:T(8,128)(2,1)} %copy.45) | copy-start | bytes 1572868
  101.4 10.2 %copy-start.16 = (f32[4,256,256]{1,2,0:T(8,128)S(1)}, f32[4,256,256]{1,2,0:T(8,128)}, u32[]{:S(2)}) copy-start(f32[4,256,256]{1,2,0:T(8,128)} %get-tuple-element.39) | copy-start | bytes 3145732
  101.4 12.2 %copy-start.5 = (f32[4,256,256]{1,2,0:T(8,128)S(1)}, f32[4,256,256]{1,2,0:T(8,128)}, u32[]{:S(2)}) copy-start(f32[4,256,256]{1,2,0:T(8,128)} %get-tuple-element.35) | copy-start | bytes 3145732
  103.9 10.7 %copy-start.1 = (f32[4,256,256]{1,2,0:T(8,128)S(1)}, f32[4,256,256]{1,2,0:T(8,128)}, u32[]{:S(2)}) copy-start(f32[4,256,256]{1,2,0:T(8,128)} %get-tuple-element.63) | copy-start | bytes 3145732
  103.9 10.7 %copy-start.11 = (f32[4,256,256]{1,2,0:T(8,128)S(1)}, f32[4,256,256]{1,2,0:T(8,128)}, u32[]{:S(2)}) copy-start(f32[4,256,256]{1,2,0:T(8,128)} %get-tuple-element.65) | copy-start | bytes 3145732
  103.9 10.7 %copy-start.13 = (f32[4,256,256]{1,2,0:T(8,128)S(1)}, f32[4,256,256]{1,2,0:T(8,128)}, u32[]{:S(2)}) copy-start(f32[4,256,256]{1,2,0:T(8,128)} %get-tuple-element.61) | copy-start | bytes 3145732
  103.9 10.7 %copy-start.21 = (f32[4,256,256]{1,2,0:T(8,128)S(1)}, f32[4,256,256]{1,2,0:T(8,128)}, u32[]{:S(2)}) copy-start(f32[4,256,256]{1,2,0:T(8,128)} %get-tuple-element.69) | copy-start | bytes 3145732
  103.9 10.7 %copy-start.24 = (f32[4,256,256]{1,2,0:T(8,128)S(1)}, f32[4,256,256]{1,2,0:T(8,128)}, u32[]{:S(2)}) copy-start(f32[4,256,256]{1,2,0:T(8,128)} %get-tuple-element.67) | copy-start | bytes 3145732
  166.9 38.0 %copy-start.43 = (f32[256]{0:T(256)S(1)}, f32[256]{0:T(256)}, u32[]{:S(2)}) copy-start(f32[256]{0:T(256)} %param.19) | copy-start | bytes 3076
  (32 other events, 175.4 us)
where the time goes:
time: 208 us; the launch traced here: 206 us
  matrix products  92.5 us (44%)
  blocking collectives  48.2 us (23%)
  starting transfers between devices  33.7 us (16%)
  local copies, waits for them, and re-layouts  22.3 us (11%)
  other arithmetic  8.96 us (4%)
    dot_general x20, matrix products, tile_scores(): jnp.einsum('qhd,khd->hqk', query_part, key_part, preferred_element_type=j...  37.4 us
    dot_general x20, matrix products, tile_values(): jnp.einsum('hqk,khd->qhd', exp_scores.astype(jnp.bfloat16), value_part, p...  35.7 us
    ppermute x12, starting transfers between devices, from_behind(): return lax.ppermute(value, axis, pairs)  33.7 us
    all_to_all x1, blocking collectives, on_device(): lax.all_to_all(outgoing, 'pack', split_axis=0, concat_axis=0, tiled=True)  27 us
    all_to_all x1, blocking collectives, on_device(): lax.all_to_all(produced, 'pack', split_axis=0, concat_axis=0, tiled=True)  21.3 us
    dot_general x1, matrix products, on_device(): jnp.einsum('sepf,efd->sepd', hidden, expert_out, preferred_element_type=j...  16.7 us
    ppermute x8, local copies, waits for them, and re-layouts, from_behind(): return lax.ppermute(value, axis, pairs)  15.6 us
    unnamed x91, local copies, waits for them, and re-layouts  6.52 us
  transfers between devices with their start and end apart: 12, of which 0 were waited for; matrix products, arithmetic and copies ran while one was open for 46% of the time, Pallas kernels for 0%

commit v1 on v0

v1 whole, which is shorter than its diff:
```python
import jax
import jax.numpy as jnp
from jax import lax
from jax.experimental import pallas as pl
from jax.experimental.pallas import tpu as pltpu
from jax.sharding import PartitionSpec as P

HEADS = 16
PACK = 32
SIDE = 4
ROWS = 256
CAP = 16
PAIRS = HEADS // 2
LANES = 128
FAR_AWAY = -1e30
MESH = pl.DeviceIdType.MESH
OWN, SIB, PREV, NEXT, FWD = range(5)


def hops(step):
    return min(step[0], SIDE - step[0]) + min(step[1], SIDE - step[1])


STEPS = sorted(
    [(dy, dx, dc) for dy in range(SIDE) for dx in range(SIDE) for dc in (1, 0)],
    key=lambda step: (-hops(step), step[0], step[1], -step[2]),
)
HALF = PACK // 2


def moved(me, step, sign):
    y, x, core = me // (2 * SIDE), (me // 2) % SIDE, me % 2
    y = lax.rem(y + sign * step[0] + SIDE, SIDE)
    x = lax.rem(x + sign * step[1] + SIDE, SIDE)
    core = lax.rem(core + step[2], 2)
    return (y * SIDE + x) * 2 + core


def kernel(
    q_hbm, k_hbm, v_hbm, res_hbm, seg_ref, route_ref, gate_ref, gain_ref, wo_hbm, w1_hbm, w2_hbm,
    out_ref,
    qs, kt, vt, segs, qaug, kaug, res, wo, w1, w2, stream, place, place_t, gate_cols,
    outg, recv, hid, prod, ret,
    load_sem, near_send, near_recv, seg_send, seg_recv, sib_send, sib_recv, fwd_send, fwd_recv,
    go_send, go_recv, back_send, back_recv,
):
    me = lax.axis_index("pack")
    core = lax.rem(me, 2)
    sibling = me + 1 - 2 * core
    after = lax.rem(me + 2, PACK)
    before = lax.rem(me + PACK - 2, PACK)
    fwd_from = NEXT - core

    barrier = pltpu.get_barrier_semaphore()

    @pl.loop(1, PACK)
    def _(d):
        pl.semaphore_signal(
            barrier, inc=1, device_id={"pack": lax.rem(me + d, PACK)}, device_id_type=MESH
        )

    loads = [
        pltpu.make_async_copy(src, dst, load_sem.at[i])
        for i, (src, dst) in enumerate(
            [
                (k_hbm, kt.at[OWN]),
                (v_hbm, vt.at[OWN]),
                (q_hbm, qs),
                (res_hbm, res),
                (wo_hbm, wo),
                (w1_hbm.at[0], w1),
                (w2_hbm.at[0], w2),
            ]
        )
    ]
    for load in loads[:4]:
        load.start()
    pl.semaphore_wait(barrier, PACK - 1)

    def cols(p):
        return pl.ds(pl.multiple_of(p * LANES, LANES), LANES)

    def remote(src, dst, send, recv_s, peer):
        return pltpu.make_async_remote_copy(
            src_ref=src, dst_ref=dst, send_sem=send, recv_sem=recv_s,
            device_id={"pack": peer}, device_id_type=MESH,
        )

    def halo(p):
        c = cols(p)
        return [
            remote(k_hbm.at[:, c], kt.at[PREV, :, c], near_send.at[0, p], near_recv.at[0, p], after),
            remote(v_hbm.at[:, c], vt.at[PREV, :, c], near_send.at[1, p], near_recv.at[1, p], after),
            remote(k_hbm.at[:, c], kt.at[NEXT, :, c], near_send.at[2, p], near_recv.at[2, p], before),
            remote(v_hbm.at[:, c], vt.at[NEXT, :, c], near_send.at[3, p], near_recv.at[3, p], before),
        ]

    def forward(p):
        c = cols(p)
        return [
            remote(kt.at[fwd_from, :, c], kt.at[FWD, :, c], fwd_send.at[0, p], fwd_recv.at[0, p], sibling),
            remote(vt.at[fwd_from, :, c], vt.at[FWD, :, c], fwd_send.at[1, p], fwd_recv.at[1, p], sibling),
        ]

    seg_out = [
        remote(seg_ref, segs.at[PREV], seg_send.at[0], seg_recv.at[0], after),
        remote(seg_ref, segs.at[NEXT], seg_send.at[1], seg_recv.at[1], before),
        remote(seg_ref, segs.at[SIB], seg_send.at[2], seg_recv.at[2], sibling),
    ]
    seg_fwd = remote(segs.at[fwd_from], segs.at[FWD], seg_send.at[3], seg_recv.at[3], sibling)
    sib_out = [
        remote(k_hbm, kt.at[SIB], sib_send.at[0], sib_recv.at[0], sibling),
        remote(v_hbm, vt.at[SIB], sib_send.at[1], sib_recv.at[1], sibling),
    ]
    for copy in seg_out + halo(0):
        copy.start()
    for copy in sib_out:
        copy.start()

    @pl.loop(1, PAIRS)
    def _(p):
        for copy in halo(p):
            copy.start()

    for load in loads[4:]:
        load.start()

    def image_rows(seg):
        spread = jnp.broadcast_to(seg[0:1, :], (LANES, ROWS))
        return spread == lax.broadcasted_iota(jnp.int32, (LANES, ROWS), 0)

    own_rows = image_rows(seg_ref[...])
    qaug[...] = jnp.where(own_rows, FAR_AWAY, 0.0).T.astype(jnp.bfloat16)
    kaug[OWN] = jnp.where(own_rows, 0.0, 1.0).T.astype(jnp.bfloat16)

    expert_of = jnp.zeros((PACK, ROWS), jnp.int32)
    place_iota = lax.broadcasted_iota(jnp.int32, (PACK, ROWS), 0)
    for j, step in enumerate(STEPS):
        expert_of = jnp.where(place_iota == j, moved(me, step, 1), expert_of)
    chosen = jnp.broadcast_to(route_ref[0:1, :], (PACK, ROWS)) == expert_of
    earlier = lax.broadcasted_iota(jnp.int32, (ROWS, ROWS), 0) < lax.broadcasted_iota(
        jnp.int32, (ROWS, ROWS), 1
    )
    rank = jnp.dot(
        jnp.where(chosen, 1.0, 0.0).astype(jnp.bfloat16),
        jnp.where(earlier, 1.0, 0.0).astype(jnp.bfloat16),
        preferred_element_type=jnp.float32,
    )
    slot = jnp.where(chosen, rank, -1.0)
    slot_iota = lax.broadcasted_iota(jnp.int32, (CAP, ROWS), 0).astype(jnp.float32)
    for j in range(PACK):
        hit = jnp.broadcast_to(slot[j : j + 1, :], (CAP, ROWS)) == slot_iota
        hit = jnp.where(hit, 1.0, 0.0)
        place[CAP * j : CAP * (j + 1), :] = hit.astype(jnp.bfloat16)
    for j in range(0, PACK * CAP, LANES):
        place_t[:, j : j + LANES] = place[j : j + LANES, :].astype(jnp.float32).T.astype(jnp.bfloat16)
    gate_cols[...] = jnp.broadcast_to(gate_ref[0:1, :], (LANES, ROWS)).T

    for copy in seg_out:
        copy.wait_recv()
    seg_fwd.start()
    for tile in (SIB, PREV, NEXT):
        kaug[tile] = jnp.where(image_rows(segs[tile]), 0.0, 1.0).T.astype(jnp.bfloat16)
    seg_fwd.wait_recv()
    kaug[FWD] = jnp.where(image_rows(segs[FWD]), 0.0, 1.0).T.astype(jnp.bfloat16)

    for load in loads[:5]:
        load.wait()
    stream[...] = res[...].astype(jnp.float32)
    for copy in sib_out:
        copy.wait_recv()

    exp_scale = float((1024 // HEADS) ** -0.5 * 1.4426950408889634)
    low_lanes = lax.broadcasted_iota(jnp.int32, (ROWS, LANES), 1) < LANES // 2
    ones = jnp.ones((ROWS, LANES), jnp.bfloat16)

    def attend(p):
        c = cols(p)
        both = qs[:, c]
        marks = qaug[...]
        heads = []
        for keep in (low_lanes, jnp.logical_not(low_lanes)):
            one = jnp.where(keep, both, jnp.zeros_like(both))
            lhs = jnp.concatenate([one, marks], axis=1)
            scores = []
            for tile in range(5):
                rhs = jnp.concatenate([kt[tile, :, c], kaug[tile]], axis=1)
                scores.append(
                    lax.dot_general(
                        lhs, rhs, (((1,), (1,)), ((), ())), preferred_element_type=jnp.float32
                    )
                )
            top = scores[0]
            for s in scores[1:]:
                top = jnp.maximum(top, s)
            top = jnp.max(top, axis=1, keepdims=True)
            summed = jnp.zeros((ROWS, 2 * LANES), jnp.float32)
            for tile in range(5):
                weights = jnp.exp2((scores[tile] - top) * exp_scale).astype(jnp.bfloat16)
                rhs = jnp.concatenate([vt[tile, :, c], ones], axis=1)
                summed = summed + jnp.dot(weights, rhs, preferred_element_type=jnp.float32)
            heads.append(summed[:, :LANES] / summed[:, LANES:])
        attended = jnp.where(low_lanes, heads[0], heads[1]).astype(jnp.bfloat16)
        stream[...] += jnp.dot(attended, wo[c, :], preferred_element_type=jnp.float32)

    def take(p):
        for copy in halo(p):
            copy.wait_recv()
        for copy in forward(p):
            copy.start()

    take(0)

    @pl.loop(1, PAIRS)
    def _(p):
        take(p)
        for copy in forward(p - 1):
            copy.wait_recv()
        attend(p - 1)

    for copy in forward(PAIRS - 1):
        copy.wait_recv()
    attend(PAIRS - 1)

    x = stream[...]
    mean = jnp.mean(x, axis=1, keepdims=True)
    centered = x - mean
    var = jnp.mean(centered * centered, axis=1, keepdims=True)
    normed = (centered * lax.rsqrt(var + 1e-6) * gain_ref[0:1, :]).astype(jnp.bfloat16)

    def block(j):
        return pl.ds(j * CAP, CAP)

    go = [
        remote(outg.at[block(j)], recv.at[block(j)], go_send.at[j], go_recv.at[j], moved(me, step, 1))
        for j, step in enumerate(STEPS[:-1])
    ]
    back = [
        remote(prod.at[block(j)], ret.at[block(j)], back_send.at[j], back_recv.at[j], moved(me, step, -1))
        for j, step in enumerate(STEPS[:-1])
    ]
    part = 128
    for start in range(0, PACK * CAP, part):
        outg[start : start + part, :] = jnp.dot(
            place[start : start + part, :], normed, preferred_element_type=jnp.float32
        ).astype(jnp.bfloat16)
        for j in range(start // CAP, min((start + part) // CAP, PACK - 1)):
            go[j].start()
    recv[(PACK - 1) * CAP :, :] = outg[(PACK - 1) * CAP :, :]

    loads[5].wait()
    loads[6].wait()
    wide = 512

    for half in range(2):
        rows = pl.ds(half * ROWS, ROWS)
        for j in range(half * HALF, min((half + 1) * HALF, PACK - 1)):
            go[j].wait_recv()

        @pl.loop(0, 2048 // wide)
        def _(n):
            c = pl.ds(pl.multiple_of(n * wide, wide), wide)
            h = jnp.dot(recv[rows, :], w1[:, c], preferred_element_type=jnp.float32)
            h = 0.5 * h * (1.0 + lax.erf(h * 0.7071067811865476))
            hid[:, c] = h.astype(jnp.bfloat16)

        @pl.loop(0, 1024 // wide)
        def _(n):
            c = pl.ds(pl.multiple_of(n * wide, wide), wide)
            prod[rows, c] = jnp.dot(
                hid[...], w2[:, c], preferred_element_type=jnp.float32
            ).astype(jnp.bfloat16)

        for j in range(half * HALF, min((half + 1) * HALF, PACK - 1)):
            back[j].start()
    ret[(PACK - 1) * CAP :, :] = prod[(PACK - 1) * CAP :, :]

    gate = jnp.concatenate([gate_cols[...]] * (1024 // LANES), axis=1)
    for j in range(HALF):
        back[j].wait_recv()
    first = jnp.dot(place_t[:, :ROWS], ret[:ROWS, :], preferred_element_type=jnp.float32)
    stream[...] += gate * first
    for j in range(HALF, PACK - 1):
        back[j].wait_recv()
    second = jnp.dot(place_t[:, ROWS:], ret[ROWS:, :], preferred_element_type=jnp.float32)
    out_ref[...] = (stream[...] + gate * second).astype(jnp.bfloat16)

    for copy in seg_out + sib_out + [seg_fwd]:
        copy.wait_send()

    @pl.loop(0, PAIRS)
    def _(p):
        for copy in halo(p) + forward(p):
            copy.wait_send()

    for copy in go + back:
        copy.wait_send()


def on_device(
    queries, keys, values, residual, segments, out_weight, norm_gain, routes, gate_prob,
    expert_in, expert_out,
):
    bf16, f32 = jnp.bfloat16, jnp.float32
    hbm = pl.BlockSpec(memory_space=pl.ANY)
    vmem = pl.BlockSpec(memory_space=pltpu.VMEM)
    rows_of = lambda row: jnp.broadcast_to(row.reshape(1, ROWS), (8, ROWS))
    dma = pltpu.SemaphoreType.DMA
    return pl.pallas_call(
        kernel,
        out_shape=jax.ShapeDtypeStruct((ROWS, 1024), bf16),
        in_specs=[hbm] * 4 + [vmem] * 4 + [hbm] * 3,
        out_specs=vmem,
        scratch_shapes=[
            pltpu.VMEM((ROWS, 1024), bf16),
            pltpu.VMEM((5, ROWS, 1024), bf16),
            pltpu.VMEM((5, ROWS, 1024), bf16),
            pltpu.VMEM((5, 8, ROWS), jnp.int32),
            pltpu.VMEM((ROWS, LANES), bf16),
            pltpu.VMEM((5, ROWS, LANES), bf16),
            pltpu.VMEM((ROWS, 1024), bf16),
            pltpu.VMEM((1024, 1024), bf16),
            pltpu.VMEM((1024, 2048), bf16),
            pltpu.VMEM((2048, 1024), bf16),
            pltpu.VMEM((ROWS, 1024), f32),
            pltpu.VMEM((PACK * CAP, ROWS), bf16),
            pltpu.VMEM((ROWS, PACK * CAP), bf16),
            pltpu.VMEM((ROWS, LANES), f32),
            pltpu.VMEM((PACK * CAP, 1024), bf16),
            pltpu.VMEM((PACK * CAP, 1024), bf16),
            pltpu.VMEM((ROWS, 2048), bf16),
            pltpu.VMEM((PACK * CAP, 1024), bf16),
            pltpu.VMEM((PACK * CAP, 1024), bf16),
            dma((7,)),
            dma((4, PAIRS)),
            dma((4, PAIRS)),
            dma((4,)),
            dma((4,)),
            dma((2,)),
            dma((2,)),
            dma((2, PAIRS)),
            dma((2, PAIRS)),
            dma((PACK,)),
            dma((PACK,)),
            dma((PACK,)),
            dma((PACK,)),
        ],
        compiler_params=pltpu.CompilerParams(
            collective_id=0, has_side_effects=True, vmem_limit_bytes=56 << 20
        ),
        name="layer",
    )(
        queries, keys, values, residual,
        rows_of(segments), rows_of(routes), rows_of(gate_prob),
        jnp.broadcast_to(norm_gain.reshape(1, 1024), (8, 1024)),
        out_weight, expert_in, expert_out,
    )


def solution(mesh):
    placed = (
        P(("dp", "pack"), None),
        P(("dp", "pack"), None),
        P(("dp", "pack"), None),
        P(("dp", "pack"), None),
        P(("dp", "pack")),
        P(),
        P(),
        P(("dp", "pack"), None),
        P(("dp", "pack")),
        P("pack", None, None),
        P("pack", None, None),
    )
    return jax.shard_map(
        on_device, mesh=mesh, in_specs=placed, out_specs=P(("dp", "pack"), None), check_vma=False
    )
```

time: 208 us -> 77.3 us (0.37)
  matrix products: 92.5 us -> 0 us
  Pallas kernels: 0 us -> 70 us
  blocking collectives: 48.2 us -> 0 us
  starting transfers between devices: 33.7 us -> 0 us
  local copies, waits for them, and re-layouts: 22.3 us -> 6.99 us
  other arithmetic: 8.96 us -> 0 us
    dot_general x44 -> x0, matrix products: 92.5 us -> none  [the longest x20 37.4 us: tile_scores(): jnp.einsum('qhd,khd->hqk', query_part, key_part, preferred_element_type=j...]
    pallas_call x0 -> x1, Pallas kernels: none -> 70 us  [on_device(): pl.pallas_call(kernel, out_shape=jax.ShapeDtypeStruct((ROWS, 1024), bf16)...]
    all_to_all x2 -> x0, blocking collectives: 48.2 us -> none  [the longest x1 27 us: on_device(): lax.all_to_all(outgoing, 'pack', split_axis=0, concat_axis=0, tiled=True)]
    ppermute x12 -> x0, starting transfers between devices: 33.7 us -> none  [from_behind(): return lax.ppermute(value, axis, pairs)]
    ppermute x8 -> x0, local copies, waits for them, and re-layouts: 15.6 us -> none  [from_behind(): return lax.ppermute(value, axis, pairs)]
    reduce_sum x6 -> x0, other arithmetic: 5.77 us -> none  [the longest x4 4.74 us: on_device(): row_total = row_total + exp_scores.sum(axis=2)]
    broadcast_in_dim x0 -> x4, local copies, waits for them, and re-layouts: none -> 5.12 us  [the longest x3 3.82 us: on_device(): rows_of = lambda row: jnp.broadcast_to(row.reshape(1, ROWS), (8, ROWS))]
    unnamed x91 -> x1, local copies, waits for them, and re-layouts: 6.52 us -> 1.87 us
  transfers between devices with their start and end apart: 12 -> 0, of which waited for: 0 -> 0; matrix products, arithmetic and copies ran while one was open for 46% -> 0% of each run, Pallas kernels for 0% -> 0%
where the time goes in v1:
time: 77.3 us; the launch traced here: 77 us
  Pallas kernels  70 us (91%)
  local copies, waits for them, and re-layouts  6.99 us (9%)
    pallas_call x1, Pallas kernels, on_device(): pl.pallas_call(kernel, out_shape=jax.ShapeDtypeStruct((ROWS, 1024), bf16)...  70 us
    broadcast_in_dim x3, local copies, waits for them, and re-layouts, on_device(): rows_of = lambda row: jnp.broadcast_to(row.reshape(1, ROWS), (8, ROWS))  3.82 us
    unnamed x1, local copies, waits for them, and re-layouts  1.87 us

profile of v1, /device:TPU:1, one launch (start us, length us, event | category | flops | bytes accessed | tf_op | source)
XLA Modules:
  0.0 77.0 jit_solution(403726455753640902)
XLA Ops:
  0.0 1.3 %broadcast_in_dim.10.seg_ref = s32[8,256]{1,0:T(8,128)} broadcast(s32[256]{0:T(256)} %param.15), dimensions={1} | broadcast | bytes 9216 | tf_op jit(solution)/shard_map/broadcast_in_dim | solution.py:307
  1.3 1.3 %broadcast_in_dim.24.route_ref = s32[8,256]{1,0:T(8,128)} broadcast(s32[256]{0:T(256)} %bitcast.1), dimensions={1} | broadcast | bytes 9216 | tf_op jit(solution)/shard_map/broadcast_in_dim | solution.py:307
  2.5 1.3 %broadcast_in_dim.25.gate_ref = f32[8,256]{1,0:T(8,128)} broadcast(f32[256]{0:T(256)} %param.19), dimensions={1} | broadcast | bytes 9216 | tf_op jit(solution)/shard_map/broadcast_in_dim | solution.py:307
  3.8 1.3 %broadcast_in_dim.26.gain_ref = f32[8,1024]{1,0:T(8,128)} broadcast(f32[1024]{0:T(1024)} %param.17), dimensions={1} | broadcast | bytes 36864 | tf_op jit(solution)/shard_map/broadcast_in_dim | solution.py:355
  5.1 70.0 %layer.1 = bf16[256,1024]{1,0:T(8,128)(2,1)} custom-call(bf16[256,1024]{1,0:T(8,128)(2,1)} %q_hbm.1, bf16[256,1024]{1,0:T(8,128)(2,1)} %k_hbm.1, bf16[256,1024]{1,0:T(8,128)(2,1)} %v_hbm.1, bf16[256,1024]{1,0:T(8,128)(2,1)} %res_hbm.1, s32[8,256]{1,0:T(8,128)} %broadcast_in_dim.10.seg_ref, s32[8,256]{1,0:T(8,128)} %broadcast_in_dim.24.route_ref, ...), custom_call_target="tpu_custom_call" | custom-call | tf_op jit(solution)/shard_map/layer/pallas_call | solution.py:309
  75.2 1.9 %copy.13 = bf16[256,1024]{1,0:T(8,128)(2,1)} copy(bf16[256,1024]{1,0:T(8,128)(2,1)} %layer.1) | data formatting | bytes 1048576

commit v2 on v1

v2 whole, which is shorter than its diff:
```python
import jax
import jax.numpy as jnp
from jax import lax
from jax.experimental import pallas as pl
from jax.experimental.pallas import tpu as pltpu
from jax.sharding import PartitionSpec as P

HEADS = 16
PACK = 32
SIDE = 4
ROWS = 256
CAP = 16
PAIRS = HEADS // 2
LANES = 128
FAR_AWAY = -1e30
MESH = pl.DeviceIdType.MESH
OWN, SIB, NEAR, FAR, FWD = range(5)
KEPT = 5
WAVES = (0, 10, 22, 32)
WIDE = 512


def hops(step):
    return min(step[0], SIDE - step[0]) + min(step[1], SIDE - step[1])


STEPS = sorted(
    [(dy, dx, dc) for dy in range(SIDE) for dx in range(SIDE) for dc in (1, 0)],
    key=lambda step: (-hops(step), step[0], step[1], -step[2]),
)
HALF = PACK // 2


def moved(me, step, sign):
    y, x, core = me // (2 * SIDE), (me // 2) % SIDE, me % 2
    y = lax.rem(y + sign * step[0] + SIDE, SIDE)
    x = lax.rem(x + sign * step[1] + SIDE, SIDE)
    core = lax.rem(core + step[2], 2)
    return (y * SIDE + x) * 2 + core


def kernel(
    q_hbm, k_hbm, v_hbm, res_hbm, seg_ref, route_ref, gate_ref, gain_ref, wo_hbm, w1_hbm, w2_hbm,
    out_ref,
    qs, kt, vt, near, fwd, pick, help_out, help_in, segs, qaug, kaug, helped, att,
    res, wo, w1, w2, stream, place, place_t, gate_cols, outg, recv, hid, prod, ret,
    load_sem, seg_send, seg_recv, sib_send, sib_recv, near_send, near_recv, fwd_send, fwd_recv,
    help_send, help_recv, go_send, go_recv, back_send, back_recv,
):
    me = lax.axis_index("pack")
    core = lax.rem(me, 2)
    sibling = me + 1 - 2 * core
    across = lax.rem(me + 2 * core + PACK - 1, PACK)

    barrier = pltpu.get_barrier_semaphore()

    @pl.loop(1, PACK)
    def _(d):
        pl.semaphore_signal(
            barrier, inc=1, device_id={"pack": lax.rem(me + d, PACK)}, device_id_type=MESH
        )

    loads = [
        pltpu.make_async_copy(src, dst, load_sem.at[i])
        for i, (src, dst) in enumerate(
            [
                (k_hbm, kt.at[OWN]),
                (v_hbm, vt.at[OWN]),
                (q_hbm, qs),
                (res_hbm, res),
                (wo_hbm, wo),
                (w1_hbm.at[0], w1),
                (w2_hbm.at[0], w2),
            ]
        )
    ]
    for load in loads[:4]:
        load.start()
    segs[OWN] = jnp.broadcast_to(seg_ref[0:1, :], (8, ROWS))
    pl.semaphore_wait(barrier, PACK - 1)

    def cols(p):
        return pl.ds(pl.multiple_of(p * LANES, LANES), LANES)

    def remote(src, dst, send, recv_s, peer):
        return pltpu.make_async_remote_copy(
            src_ref=src, dst_ref=dst, send_sem=send, recv_sem=recv_s,
            device_id={"pack": peer}, device_id_type=MESH,
        )

    def plain(p):
        return [
            remote(hbm.at[:, cols(p)], near.at[2 * p + i], near_send.at[2 * p + i], near_recv.at[2 * p + i], across)
            for i, hbm in enumerate((k_hbm, v_hbm))
        ]

    def picked(n):
        at = 2 * KEPT + n
        return remote(pick.at[n], near.at[at], near_send.at[at], near_recv.at[at], across)

    def forward(n):
        return remote(near.at[n], fwd.at[n], fwd_send.at[n], fwd_recv.at[n], sibling)

    def helping(n):
        return remote(help_out.at[n], help_in.at[n], help_send.at[n], help_recv.at[n], across)

    seg_out = [
        remote(segs.at[OWN], segs.at[NEAR], seg_send.at[0], seg_recv.at[0], across),
        remote(segs.at[OWN], segs.at[SIB], seg_send.at[1], seg_recv.at[1], sibling),
    ]
    seg_on = [
        remote(segs.at[SIB], segs.at[FAR], seg_send.at[2], seg_recv.at[2], across),
        remote(segs.at[NEAR], segs.at[FWD], seg_send.at[3], seg_recv.at[3], sibling),
    ]
    first, rest = pl.ds(0, KEPT * LANES), pl.ds(KEPT * LANES, (PAIRS - KEPT) * LANES)
    sib_out = [
        remote(hbm.at[:, c], tile.at[SIB, :, c], sib_send.at[i, n], sib_recv.at[i, n], sibling)
        for n, c in enumerate((first, rest))
        for i, (hbm, tile) in enumerate(((k_hbm, kt), (v_hbm, vt)))
    ]
    for copy in seg_out + plain(0) + sib_out:
        copy.start()

    def edge(row, at_end):
        return jnp.where(at_end, row[:, ROWS - 1 :], row[:, :1])

    for copy in seg_out:
        copy.wait_recv()
    for copy in seg_on:
        copy.start()
    for load in loads[:4]:
        load.wait()
    for copy in sib_out[:2]:
        copy.wait_recv()
    last = core == 1
    sib_edge = edge(segs[SIB, 0:1, :], last)
    near_edge = edge(segs[NEAR, 0:1, :], core == 0)
    own_edge = edge(segs[OWN, 0:1, :], last)
    wide_here = jnp.broadcast_to(sib_edge, (ROWS, LANES)) == jnp.broadcast_to(near_edge, (ROWS, LANES))
    usual = [(t.at[OWN], p) for p in range(KEPT, PAIRS) for t in (kt, vt)]
    usual += [(qs, p) for p in range(KEPT, PAIRS)]
    for n in range(2 * KEPT):
        wide = (kt, vt)[n % 2][SIB, :, LANES * (n // 2) : LANES * (n // 2 + 1)]
        if n < len(usual):
            src, p = usual[n]
            wide = jnp.where(wide_here, wide, src[:, LANES * p : LANES * (p + 1)])
        pick[n] = wide
        picked(n).start()

    @pl.loop(1, KEPT)
    def _(p):
        for copy in plain(p):
            copy.start()

    for load in loads[4:]:
        load.start()

    def image_rows(seg):
        spread = jnp.broadcast_to(seg[0:1, :], (LANES, ROWS))
        return spread == lax.broadcasted_iota(jnp.int32, (LANES, ROWS), 0)

    def query_marks(rows):
        return jnp.where(rows, FAR_AWAY, 0.0).T.astype(jnp.bfloat16)

    def key_marks(rows):
        return jnp.where(rows, 0.0, 1.0).T.astype(jnp.bfloat16)

    own_rows, near_rows = image_rows(segs[OWN]), image_rows(segs[NEAR])
    qaug[0] = query_marks(own_rows)
    qaug[1] = query_marks(near_rows)
    kaug[OWN] = key_marks(own_rows)
    kaug[NEAR] = key_marks(near_rows)
    kaug[SIB] = key_marks(image_rows(segs[SIB]))
    for copy in seg_on:
        copy.wait_recv()
    kaug[FWD] = key_marks(image_rows(segs[FWD]))
    far_edge = edge(segs[FAR, 0:1, :], core == 0)
    wide_there = jnp.broadcast_to(far_edge, (LANES, ROWS)) == jnp.broadcast_to(own_edge, (LANES, ROWS))
    kaug[FAR] = key_marks(jnp.logical_and(wide_there, image_rows(segs[FAR])))
    in_crossing = jnp.broadcast_to(segs[OWN, 0:1, :], (LANES, ROWS)) == jnp.broadcast_to(own_edge, (LANES, ROWS))
    helped[...] = jnp.where(jnp.logical_and(wide_there, in_crossing), 1.0, 0.0).T

    expert_of = jnp.zeros((PACK, ROWS), jnp.int32)
    place_iota = lax.broadcasted_iota(jnp.int32, (PACK, ROWS), 0)
    for j, step in enumerate(STEPS):
        expert_of = jnp.where(place_iota == j, moved(me, step, 1), expert_of)
    chosen = jnp.broadcast_to(route_ref[0:1, :], (PACK, ROWS)) == expert_of
    earlier = lax.broadcasted_iota(jnp.int32, (ROWS, ROWS), 0) < lax.broadcasted_iota(
        jnp.int32, (ROWS, ROWS), 1
    )
    rank = jnp.dot(
        jnp.where(chosen, 1.0, 0.0).astype(jnp.bfloat16),
        jnp.where(earlier, 1.0, 0.0).astype(jnp.bfloat16),
        preferred_element_type=jnp.float32,
    )
    slot = jnp.where(chosen, rank, -1.0)
    slot_iota = lax.broadcasted_iota(jnp.int32, (CAP, ROWS), 0).astype(jnp.float32)
    for j in range(PACK):
        hit = jnp.broadcast_to(slot[j : j + 1, :], (CAP, ROWS)) == slot_iota
        hit = jnp.where(hit, 1.0, 0.0)
        place[CAP * j : CAP * (j + 1), :] = hit.astype(jnp.bfloat16)
    for j in range(0, PACK * CAP, LANES):
        place_t[:, j : j + LANES] = place[j : j + LANES, :].astype(jnp.float32).T.astype(jnp.bfloat16)
    gate_cols[...] = jnp.broadcast_to(gate_ref[0:1, :], (LANES, ROWS)).T
    stream[...] = res[...].astype(jnp.float32)

    exp_scale = float((1024 // HEADS) ** -0.5 * 1.4426950408889634)
    low_lanes = lax.broadcasted_iota(jnp.int32, (ROWS, LANES), 1) < LANES // 2
    ones = jnp.ones((ROWS, LANES), jnp.bfloat16)

    def two_heads(both, marks, tiles):
        heads = []
        for keep in (low_lanes, jnp.logical_not(low_lanes)):
            one = jnp.where(keep, both, jnp.zeros_like(both))
            lhs = jnp.concatenate([one, marks], axis=1)
            scores = []
            for key, mark, _ in tiles:
                rhs = jnp.concatenate([key(), mark()], axis=1)
                scores.append(
                    lax.dot_general(
                        lhs, rhs, (((1,), (1,)), ((), ())), preferred_element_type=jnp.float32
                    )
                )
            top = scores[0]
            for s in scores[1:]:
                top = jnp.maximum(top, s)
            top = jnp.max(top, axis=1, keepdims=True)
            summed = jnp.zeros((ROWS, 2 * LANES), jnp.float32)
            for s, (_, _, value) in zip(scores, tiles):
                weights = jnp.exp2((s - top) * exp_scale).astype(jnp.bfloat16)
                rhs = jnp.concatenate([value(), ones], axis=1)
                summed = summed + jnp.dot(weights, rhs, preferred_element_type=jnp.float32)
            heads.append(summed[:, :LANES] / summed[:, LANES:])
        return jnp.where(low_lanes, heads[0], heads[1]).astype(jnp.bfloat16)

    def at_home(p, place_of):
        return (lambda: kt[place_of, :, cols(p)], lambda: kaug[place_of], lambda: vt[place_of, :, cols(p)])

    def arrived(buf, at, place_of):
        return (lambda: buf[at], lambda: kaug[place_of], lambda: buf[at + 1])

    def attend(p, with_far):
        tiles = [at_home(p, OWN), at_home(p, SIB), arrived(near, 2 * p, NEAR), arrived(fwd, 2 * p, FWD)]
        if with_far:
            tiles.append(arrived(near, 2 * KEPT + 2 * p, FAR))
        return two_heads(qs[:, cols(p)], qaug[0], tiles)

    for copy in sib_out[2:]:
        copy.wait_recv()
    for copy in plain(0):
        copy.wait_recv()
    for n in range(2):
        forward(n).start()
    for n in range(2 * KEPT):
        picked(n).wait_recv()
        if n < 2 * (PAIRS - KEPT):
            forward(2 * KEPT + n).start()

    @pl.loop(KEPT, PAIRS)
    def _(p):
        tiles = [at_home(p, OWN), at_home(p, SIB), arrived(near, 2 * p, NEAR)]
        help_out[p - KEPT] = two_heads(near[2 * PAIRS + p - KEPT], qaug[1], tiles)
        helping(p - KEPT).start()

    @pl.loop(KEPT, PAIRS)
    def _(p):
        forward(2 * p).wait_recv()
        forward(2 * p + 1).wait_recv()
        att[:, cols(p)] = attend(p, False)

    loads[4].wait()

    @pl.loop(0, KEPT)
    def _(p):
        @pl.when(p < KEPT - 1)
        def _():
            for n, copy in enumerate(plain(p + 1)):
                copy.wait_recv()
                forward(2 * p + 2 + n).start()

        forward(2 * p).wait_recv()
        forward(2 * p + 1).wait_recv()
        stream[...] += jnp.dot(attend(p, True), wo[cols(p), :], preferred_element_type=jnp.float32)

    for n in range(PAIRS - KEPT):
        helping(n).wait_recv()
        c = slice((KEPT + n) * LANES, (KEPT + n + 1) * LANES)
        att[:, c] = jnp.where(helped[...] > 0.5, help_in[n], att[:, c])

    x = stream[...] + jnp.dot(
        att[:, KEPT * LANES :], wo[KEPT * LANES :, :], preferred_element_type=jnp.float32
    )
    stream[...] = x
    mean = jnp.mean(x, axis=1, keepdims=True)
    centered = x - mean
    var = jnp.mean(centered * centered, axis=1, keepdims=True)
    normed = (centered * lax.rsqrt(var + 1e-6) * gain_ref[0:1, :]).astype(jnp.bfloat16)

    def block(j):
        return pl.ds(j * CAP, CAP)

    go = [
        remote(outg.at[block(j)], recv.at[block(j)], go_send.at[j], go_recv.at[j], moved(me, step, 1))
        for j, step in enumerate(STEPS[:-1])
    ]
    back = [
        remote(prod.at[block(j)], ret.at[block(j)], back_send.at[j], back_recv.at[j], moved(me, step, -1))
        for j, step in enumerate(STEPS[:-1])
    ]
    part = 128
    for start in range(0, PACK * CAP, part):
        outg[start : start + part, :] = jnp.dot(
            place[start : start + part, :], normed, preferred_element_type=jnp.float32
        ).astype(jnp.bfloat16)
        for j in range(start // CAP, min((start + part) // CAP, PACK - 1)):
            go[j].start()
    recv[(PACK - 1) * CAP :, :] = outg[(PACK - 1) * CAP :, :]

    loads[5].wait()
    loads[6].wait()

    for begin, end in zip(WAVES, WAVES[1:]):
        rows, count = pl.ds(begin * CAP, (end - begin) * CAP), (end - begin) * CAP
        for j in range(begin, min(end, PACK - 1)):
            go[j].wait_recv()

        @pl.loop(0, 2048 // WIDE)
        def _(n):
            c = pl.ds(pl.multiple_of(n * WIDE, WIDE), WIDE)
            h = jnp.dot(recv[rows, :], w1[:, c], preferred_element_type=jnp.float32)
            h = 0.5 * h * (1.0 + lax.erf(h * 0.7071067811865476))
            hid[:count, c] = h.astype(jnp.bfloat16)

        @pl.loop(0, 1024 // WIDE)
        def _(n):
            c = pl.ds(pl.multiple_of(n * WIDE, WIDE), WIDE)
            prod[rows, c] = jnp.dot(
                hid[:count, :], w2[:, c], preferred_element_type=jnp.float32
            ).astype(jnp.bfloat16)

        for j in range(begin, min(end, PACK - 1)):
            back[j].start()
    ret[(PACK - 1) * CAP :, :] = prod[(PACK - 1) * CAP :, :]

    gate = jnp.concatenate([gate_cols[...]] * (1024 // LANES), axis=1)
    for j in range(HALF):
        back[j].wait_recv()
    stream[...] += gate * jnp.dot(place_t[:, :ROWS], ret[:ROWS, :], preferred_element_type=jnp.float32)
    for j in range(HALF, PACK - 1):
        back[j].wait_recv()
    second = jnp.dot(place_t[:, ROWS:], ret[ROWS:, :], preferred_element_type=jnp.float32)
    out_ref[...] = (stream[...] + gate * second).astype(out_ref.dtype)

    for copy in seg_out + seg_on + sib_out:
        copy.wait_send()

    @pl.loop(0, KEPT)
    def _(p):
        for copy in plain(p):
            copy.wait_send()

    @pl.loop(0, 2 * KEPT)
    def _(n):
        picked(n).wait_send()

    @pl.loop(0, 2 * PAIRS)
    def _(n):
        forward(n).wait_send()

    for n in range(PAIRS - KEPT):
        helping(n).wait_send()
    for copy in go + back:
        copy.wait_send()


def on_device(
    queries, keys, values, residual, segments, out_weight, norm_gain, routes, gate_prob,
    expert_in, expert_out,
):
    bf16, f32 = jnp.bfloat16, jnp.float32
    hbm = pl.BlockSpec(memory_space=pl.ANY)
    vmem = pl.BlockSpec(memory_space=pltpu.VMEM)
    row = lambda vector: vector.reshape(1, -1)
    dma = pltpu.SemaphoreType.DMA
    return pl.pallas_call(
        kernel,
        out_shape=jax.ShapeDtypeStruct((ROWS, 1024), bf16),
        in_specs=[hbm] * 4 + [vmem] * 4 + [hbm] * 3,
        out_specs=vmem,
        scratch_shapes=[
            pltpu.VMEM((ROWS, 1024), bf16),
            pltpu.VMEM((2, ROWS, 1024), bf16),
            pltpu.VMEM((2, ROWS, 1024), bf16),
            pltpu.VMEM((4 * KEPT, ROWS, LANES), bf16),
            pltpu.VMEM((2 * PAIRS, ROWS, LANES), bf16),
            pltpu.VMEM((2 * KEPT, ROWS, LANES), bf16),
            pltpu.VMEM((PAIRS - KEPT, ROWS, LANES), bf16),
            pltpu.VMEM((PAIRS - KEPT, ROWS, LANES), bf16),
            pltpu.VMEM((5, 8, ROWS), jnp.int32),
            pltpu.VMEM((2, ROWS, LANES), bf16),
            pltpu.VMEM((5, ROWS, LANES), bf16),
            pltpu.VMEM((ROWS, LANES), f32),
            pltpu.VMEM((ROWS, 1024), bf16),
            pltpu.VMEM((ROWS, 1024), bf16),
            pltpu.VMEM((1024, 1024), bf16),
            pltpu.VMEM((1024, 2048), bf16),
            pltpu.VMEM((2048, 1024), bf16),
            pltpu.VMEM((ROWS, 1024), f32),
            pltpu.VMEM((PACK * CAP, ROWS), bf16),
            pltpu.VMEM((ROWS, PACK * CAP), bf16),
            pltpu.VMEM((ROWS, LANES), f32),
            pltpu.VMEM((PACK * CAP, 1024), bf16),
            pltpu.VMEM((PACK * CAP, 1024), bf16),
            pltpu.VMEM((ROWS, 2048), bf16),
            pltpu.VMEM((PACK * CAP, 1024), bf16),
            pltpu.VMEM((PACK * CAP, 1024), bf16),
            dma((7,)),
            dma((4,)),
            dma((4,)),
            dma((2, 2)),
            dma((2, 2)),
            dma((4 * KEPT,)),
            dma((4 * KEPT,)),
            dma((2 * PAIRS,)),
            dma((2 * PAIRS,)),
            dma((PAIRS - KEPT,)),
            dma((PAIRS - KEPT,)),
            dma((PACK,)),
            dma((PACK,)),
            dma((PACK,)),
            dma((PACK,)),
        ],
        compiler_params=pltpu.CompilerParams(
            collective_id=0, has_side_effects=True, vmem_limit_bytes=56 << 20
        ),
        name="layer",
    )(
        queries, keys, values, residual,
        row(segments), row(routes), row(gate_prob), row(norm_gain),
        out_weight, expert_in, expert_out,
    )


def solution(mesh):
    placed = (
        P(("dp", "pack"), None),
        P(("dp", "pack"), None),
        P(("dp", "pack"), None),
        P(("dp", "pack"), None),
        P(("dp", "pack")),
        P(),
        P(),
        P(("dp", "pack"), None),
        P(("dp", "pack")),
        P("pack", None, None),
        P("pack", None, None),
    )
    return jax.shard_map(
        on_device, mesh=mesh, in_specs=placed, out_specs=P(("dp", "pack"), None), check_vma=False
    )
```

time: 77.3 us -> 68.8 us (0.89)
  local copies, waits for them, and re-layouts: 6.99 us -> 1.87 us
  Pallas kernels: 70 us -> 66.8 us
    broadcast_in_dim x4 -> x0, local copies, waits for them, and re-layouts: 5.12 us -> none  [the longest x3 3.82 us: on_device(): rows_of = lambda row: jnp.broadcast_to(row.reshape(1, ROWS), (8, ROWS))]
    pallas_call x1, Pallas kernels: 70 us -> 66.8 us  [on_device(): pl.pallas_call(kernel, out_shape=jax.ShapeDtypeStruct((ROWS, 1024), bf16)...]
where the time goes in v2:
time: 68.8 us; the launch traced here: 68.7 us
  Pallas kernels  66.8 us (97%)
  local copies, waits for them, and re-layouts  1.87 us (3%)
    pallas_call x1, Pallas kernels, on_device(): pl.pallas_call(kernel, out_shape=jax.ShapeDtypeStruct((ROWS, 1024), bf16)...  66.8 us
    unnamed x1, local copies, waits for them, and re-layouts  1.87 us

profile of v2, /device:TPU:1, one launch (start us, length us, event | category | flops | bytes accessed | tf_op | source)
XLA Modules:
  0.0 68.7 jit_solution(15896611892750161180)
XLA Ops:
  0.0 66.8 %layer.1 = bf16[256,1024]{1,0:T(8,128)(2,1)} custom-call(bf16[256,1024]{1,0:T(8,128)(2,1)} %q_hbm.1, bf16[256,1024]{1,0:T(8,128)(2,1)} %k_hbm.1, bf16[256,1024]{1,0:T(8,128)(2,1)} %v_hbm.1, bf16[256,1024]{1,0:T(8,128)(2,1)} %res_hbm.1, s32[1,256]{1,0:T(1,128)} %bitcast.5, s32[1,256]{1,0:T(1,128)} %bitcast.6, f32[1,256]{1,0:T(1,128)} %bitcast.7, ...), custom_call_target="tpu_custom_call" | custom-call | tf_op jit(solution)/shard_map/layer/pallas_call | solution.py:385
  66.8 1.9 %copy.13 = bf16[256,1024]{1,0:T(8,128)(2,1)} copy(bf16[256,1024]{1,0:T(8,128)(2,1)} %layer.1) | data formatting | bytes 1048576

commit v3 on v2

--- a/solution.py
+++ b/solution.py
@@ -16,8 +16,14 @@
 MESH = pl.DeviceIdType.MESH
 OWN, SIB, NEAR, FAR, FWD = range(5)
 KEPT = 5
-WAVES = (0, 10, 22, 32)
-WIDE = 512
+WAVES = (0, 8, 20, 32)
+WIDE = 1024
+AHEAD = 1
+PICK_ORDER = (0, 1, 6, 2, 3, 7, 4, 5, 8, 9)
+UNITS = (
+    ("help", 5), ("home", 5), ("home", 0), ("help", 6), ("home", 6), ("home", 1),
+    ("help", 7), ("home", 7), ("home", 2), ("home", 3), ("home", 4),
+)
 
 
 def hops(step):
@@ -42,7 +48,8 @@
 def kernel(
     q_hbm, k_hbm, v_hbm, res_hbm, seg_ref, route_ref, gate_ref, gain_ref, wo_hbm, w1_hbm, w2_hbm,
     out_ref,
-    qs, kt, vt, near, fwd, pick, help_out, help_in, segs, qaug, kaug, helped, att,
+    qs, kt, vt, near, fwd, pick, help_out, help_in, held_a, held_b, tops_a, tops_b,
+    segs, qaug, kaug, helped, att,
     res, wo, w1, w2, stream, place, place_t, gate_cols, outg, recv, hid, prod, ret,
     load_sem, seg_send, seg_recv, sib_send, sib_recv, near_send, near_recv, fwd_send, fwd_recv,
     help_send, help_recv, go_send, go_recv, back_send, back_recv,
@@ -118,7 +125,7 @@
         for n, c in enumerate((first, rest))
         for i, (hbm, tile) in enumerate(((k_hbm, kt), (v_hbm, vt)))
     ]
-    for copy in seg_out + plain(0) + sib_out:
+    for copy in seg_out + plain(0) + sib_out + plain(1):
         copy.start()
 
     def edge(row, at_end):
@@ -145,9 +152,11 @@
             src, p = usual[n]
             wide = jnp.where(wide_here, wide, src[:, LANES * p : LANES * (p + 1)])
         pick[n] = wide
+
+    for n in PICK_ORDER:
         picked(n).start()
 
-    @pl.loop(1, KEPT)
+    @pl.loop(2, KEPT)
     def _(p):
         for copy in plain(p):
             copy.start()
@@ -208,79 +217,100 @@
     low_lanes = lax.broadcasted_iota(jnp.int32, (ROWS, LANES), 1) < LANES // 2
     ones = jnp.ones((ROWS, LANES), jnp.bfloat16)
 
-    def two_heads(both, marks, tiles):
-        heads = []
-        for keep in (low_lanes, jnp.logical_not(low_lanes)):
-            one = jnp.where(keep, both, jnp.zeros_like(both))
-            lhs = jnp.concatenate([one, marks], axis=1)
-            scores = []
-            for key, mark, _ in tiles:
-                rhs = jnp.concatenate([key(), mark()], axis=1)
-                scores.append(
-                    lax.dot_general(
-                        lhs, rhs, (((1,), (1,)), ((), ())), preferred_element_type=jnp.float32
-                    )
-                )
-            top = scores[0]
-            for s in scores[1:]:
-                top = jnp.maximum(top, s)
-            top = jnp.max(top, axis=1, keepdims=True)
-            summed = jnp.zeros((ROWS, 2 * LANES), jnp.float32)
-            for s, (_, _, value) in zip(scores, tiles):
-                weights = jnp.exp2((s - top) * exp_scale).astype(jnp.bfloat16)
-                rhs = jnp.concatenate([value(), ones], axis=1)
-                summed = summed + jnp.dot(weights, rhs, preferred_element_type=jnp.float32)
-            heads.append(summed[:, :LANES] / summed[:, LANES:])
-        return jnp.where(low_lanes, heads[0], heads[1]).astype(jnp.bfloat16)
-
     def at_home(p, place_of):
-        return (lambda: kt[place_of, :, cols(p)], lambda: kaug[place_of], lambda: vt[place_of, :, cols(p)])
+        c = slice(p * LANES, (p + 1) * LANES)
+        return (lambda: kt[place_of, :, c], lambda: kaug[place_of], lambda: vt[place_of, :, c])
 
     def arrived(buf, at, place_of):
         return (lambda: buf[at], lambda: kaug[place_of], lambda: buf[at + 1])
 
-    def attend(p, with_far):
-        tiles = [at_home(p, OWN), at_home(p, SIB), arrived(near, 2 * p, NEAR), arrived(fwd, 2 * p, FWD)]
-        if with_far:
-            tiles.append(arrived(near, 2 * KEPT + 2 * p, FAR))
-        return two_heads(qs[:, cols(p)], qaug[0], tiles)
-
+    def tiles_of(kind, p):
+        tiles = [at_home(p, OWN), at_home(p, SIB), arrived(near, 2 * p, NEAR)]
+        if kind == "home":
+            tiles.append(arrived(fwd, 2 * p, FWD))
+            if p < KEPT:
+                tiles.append(arrived(near, 2 * KEPT + 2 * p, FAR))
+        return tiles
+
+    def begin_unit(kind, p, held, tops):
+        if kind == "home":
+            both, marks = qs[:, p * LANES : (p + 1) * LANES], qaug[0]
+        else:
+            both, marks = near[2 * PAIRS + p - KEPT], qaug[1]
+        zero = jnp.zeros_like(both)
+        lhs = jnp.concatenate(
+            [
+                jnp.concatenate([jnp.where(low_lanes, both, zero), marks], axis=1),
+                jnp.concatenate([jnp.where(low_lanes, zero, both), marks], axis=1),
+            ],
+            axis=0,
+        )
+        top = None
+        for n, (key, mark, _) in enumerate(tiles_of(kind, p)):
+            scores = lax.dot_general(
+                lhs,
+                jnp.concatenate([key(), mark()], axis=1),
+                (((1,), (1,)), ((), ())),
+                preferred_element_type=jnp.float32,
+            )
+            held[n] = scores
+            top = scores if top is None else jnp.maximum(top, scores)
+        tops[...] = jnp.broadcast_to(jnp.max(top, axis=1, keepdims=True), (2 * ROWS, LANES))
+
+    def finish_unit(kind, p, held, tops):
+        top = jnp.concatenate([tops[...], tops[...]], axis=1)
+        summed = jnp.zeros((2 * ROWS, 2 * LANES), jnp.float32)
+        for n, (_, _, value) in enumerate(tiles_of(kind, p)):
+            weights = jnp.exp2((held[n] - top) * exp_scale).astype(jnp.bfloat16)
+            rhs = jnp.concatenate([value(), ones], axis=1)
+            summed = summed + jnp.dot(weights, rhs, preferred_element_type=jnp.float32)
+        both = summed[:, :LANES] / summed[:, LANES:]
+        attended = jnp.where(low_lanes, both[:ROWS], both[ROWS:]).astype(jnp.bfloat16)
+        if kind == "help":
+            help_out[p - KEPT] = attended
+            helping(p - KEPT).start()
+        elif p >= KEPT:
+            att[:, p * LANES : (p + 1) * LANES] = attended
+        else:
+            stream[...] += jnp.dot(
+                attended, wo[p * LANES : (p + 1) * LANES, :], preferred_element_type=jnp.float32
+            )
+
+    came = set()
+
+    def near_came(at):
+        if at not in came:
+            came.add(at)
+            copy = plain(at // 2)[at % 2] if at < 2 * KEPT else picked(at - 2 * KEPT)
+            copy.wait_recv()
+            if at < 2 * PAIRS:
+                forward(at).start()
+
+    def unit_came(kind, p):
+        near_came(2 * p)
+        near_came(2 * p + 1)
+        if kind == "help":
+            near_came(2 * PAIRS + p - KEPT)
+        elif p < KEPT:
+            near_came(2 * KEPT + 2 * p)
+            near_came(2 * KEPT + 2 * p + 1)
+
+    for at in range(4):
+        near_came(at)
     for copy in sib_out[2:]:
         copy.wait_recv()
-    for copy in plain(0):
-        copy.wait_recv()
-    for n in range(2):
-        forward(n).start()
-    for n in range(2 * KEPT):
-        picked(n).wait_recv()
-        if n < 2 * (PAIRS - KEPT):
-            forward(2 * KEPT + n).start()
-
-    @pl.loop(KEPT, PAIRS)
-    def _(p):
-        tiles = [at_home(p, OWN), at_home(p, SIB), arrived(near, 2 * p, NEAR)]
-        help_out[p - KEPT] = two_heads(near[2 * PAIRS + p - KEPT], qaug[1], tiles)
-        helping(p - KEPT).start()
-
-    @pl.loop(KEPT, PAIRS)
-    def _(p):
-        forward(2 * p).wait_recv()
-        forward(2 * p + 1).wait_recv()
-        att[:, cols(p)] = attend(p, False)
-
     loads[4].wait()
-
-    @pl.loop(0, KEPT)
-    def _(p):
-        @pl.when(p < KEPT - 1)
-        def _():
-            for n, copy in enumerate(plain(p + 1)):
-                copy.wait_recv()
-                forward(2 * p + 2 + n).start()
-
-        forward(2 * p).wait_recv()
-        forward(2 * p + 1).wait_recv()
-        stream[...] += jnp.dot(attend(p, True), wo[cols(p), :], preferred_element_type=jnp.float32)
+    stages = ((held_a, tops_a), (held_b, tops_b))
+    for n, unit in enumerate(UNITS):
+        for later in UNITS[n : n + 1 + AHEAD]:
+            unit_came(*later)
+        if unit[0] == "home":
+            forward(2 * unit[1]).wait_recv()
+            forward(2 * unit[1] + 1).wait_recv()
+        begin_unit(*unit, *stages[n % 2])
+        if n:
+            finish_unit(*UNITS[n - 1], *stages[(n - 1) % 2])
+    finish_unit(*UNITS[-1], *stages[(len(UNITS) - 1) % 2])
 
     for n in range(PAIRS - KEPT):
         helping(n).wait_recv()
@@ -396,6 +426,10 @@
             pltpu.VMEM((2 * KEPT, ROWS, LANES), bf16),
             pltpu.VMEM((PAIRS - KEPT, ROWS, LANES), bf16),
             pltpu.VMEM((PAIRS - KEPT, ROWS, LANES), bf16),
+            pltpu.VMEM((5, 2 * ROWS, ROWS), f32),
+            pltpu.VMEM((5, 2 * ROWS, ROWS), f32),
+            pltpu.VMEM((2 * ROWS, LANES), f32),
+            pltpu.VMEM((2 * ROWS, LANES), f32),
             pltpu.VMEM((5, 8, ROWS), jnp.int32),
             pltpu.VMEM((2, ROWS, LANES), bf16),
             pltpu.VMEM((5, ROWS, LANES), bf16),

time: 68.8 us -> 63.8 us (0.927)
  Pallas kernels: 66.8 us -> 61.8 us
    pallas_call x1, Pallas kernels: 66.8 us -> 61.8 us  [on_device(): pl.pallas_call(kernel, out_shape=jax.ShapeDtypeStruct((ROWS, 1024), bf16)...]
where the time goes in v3:
time: 63.8 us; the launch traced here: 63.7 us
  Pallas kernels  61.8 us (97%)
  local copies, waits for them, and re-layouts  1.87 us (3%)
    pallas_call x1, Pallas kernels, on_device(): pl.pallas_call(kernel, out_shape=jax.ShapeDtypeStruct((ROWS, 1024), bf16)...  61.8 us
    unnamed x1, local copies, waits for them, and re-layouts  1.87 us

profile of v3, /device:TPU:1, one launch (start us, length us, event | category | flops | bytes accessed | tf_op | source)
XLA Modules:
  0.0 63.7 jit_solution(11496148424482841328)
XLA Ops:
  0.0 61.8 %layer.1 = bf16[256,1024]{1,0:T(8,128)(2,1)} custom-call(bf16[256,1024]{1,0:T(8,128)(2,1)} %q_hbm.1, bf16[256,1024]{1,0:T(8,128)(2,1)} %k_hbm.1, bf16[256,1024]{1,0:T(8,128)(2,1)} %v_hbm.1, bf16[256,1024]{1,0:T(8,128)(2,1)} %res_hbm.1, s32[1,256]{1,0:T(1,128)} %bitcast.5, s32[1,256]{1,0:T(1,128)} %bitcast.6, f32[1,256]{1,0:T(1,128)} %bitcast.7, ...), custom_call_target="tpu_custom_call" | custom-call | tf_op jit(solution)/shard_map/layer/pallas_call | solution.py:415
  61.8 1.9 %copy.13 = bf16[256,1024]{1,0:T(8,128)(2,1)} copy(bf16[256,1024]{1,0:T(8,128)(2,1)} %layer.1) | data formatting | bytes 1048576

commit v4 on v3

--- a/solution.py
+++ b/solution.py
@@ -20,7 +20,7 @@
 WIDE = 1024
 AHEAD = 1
 PICK_ORDER = (0, 1, 6, 2, 3, 7, 4, 5, 8, 9)
-UNITS = (
+UNITS = tuple(("part", pair) for pair in range(PAIRS)) + (
     ("help", 5), ("home", 5), ("home", 0), ("help", 6), ("home", 6), ("home", 1),
     ("help", 7), ("home", 7), ("home", 2), ("home", 3), ("home", 4),
 )
@@ -48,7 +48,7 @@
 def kernel(
     q_hbm, k_hbm, v_hbm, res_hbm, seg_ref, route_ref, gate_ref, gain_ref, wo_hbm, w1_hbm, w2_hbm,
     out_ref,
-    qs, kt, vt, near, fwd, pick, help_out, help_in, held_a, held_b, tops_a, tops_b,
+    qs, kt, vt, near, fwd, pick, help_out, help_in, held_a, held_b, tops_a, tops_b, parts, part_tops,
     segs, qaug, kaug, helped, att,
     res, wo, w1, w2, stream, place, place_t, gate_cols, outg, recv, hid, prod, ret,
     load_sem, seg_send, seg_recv, sib_send, sib_recv, near_send, near_recv, fwd_send, fwd_recv,
@@ -127,6 +127,29 @@
     ]
     for copy in seg_out + plain(0) + sib_out + plain(1):
         copy.start()
+
+    expert_of = jnp.zeros((PACK, ROWS), jnp.int32)
+    place_iota = lax.broadcasted_iota(jnp.int32, (PACK, ROWS), 0)
+    for j, step in enumerate(STEPS):
+        expert_of = jnp.where(place_iota == j, moved(me, step, 1), expert_of)
+    chosen = jnp.broadcast_to(route_ref[0:1, :], (PACK, ROWS)) == expert_of
+    earlier = lax.broadcasted_iota(jnp.int32, (ROWS, ROWS), 0) < lax.broadcasted_iota(
+        jnp.int32, (ROWS, ROWS), 1
+    )
+    rank = jnp.dot(
+        jnp.where(chosen, 1.0, 0.0).astype(jnp.bfloat16),
+        jnp.where(earlier, 1.0, 0.0).astype(jnp.bfloat16),
+        preferred_element_type=jnp.float32,
+    )
+    slot = jnp.where(chosen, rank, -1.0)
+    slot_iota = lax.broadcasted_iota(jnp.int32, (CAP, ROWS), 0).astype(jnp.float32)
+    for j in range(PACK):
+        hit = jnp.broadcast_to(slot[j : j + 1, :], (CAP, ROWS)) == slot_iota
+        hit = jnp.where(hit, 1.0, 0.0)
+        place[CAP * j : CAP * (j + 1), :] = hit.astype(jnp.bfloat16)
+    for j in range(0, PACK * CAP, LANES):
+        place_t[:, j : j + LANES] = place[j : j + LANES, :].astype(jnp.float32).T.astype(jnp.bfloat16)
+    gate_cols[...] = jnp.broadcast_to(gate_ref[0:1, :], (LANES, ROWS)).T
 
     def edge(row, at_end):
         return jnp.where(at_end, row[:, ROWS - 1 :], row[:, :1])
@@ -180,39 +203,6 @@
     kaug[OWN] = key_marks(own_rows)
     kaug[NEAR] = key_marks(near_rows)
     kaug[SIB] = key_marks(image_rows(segs[SIB]))
-    for copy in seg_on:
-        copy.wait_recv()
-    kaug[FWD] = key_marks(image_rows(segs[FWD]))
-    far_edge = edge(segs[FAR, 0:1, :], core == 0)
-    wide_there = jnp.broadcast_to(far_edge, (LANES, ROWS)) == jnp.broadcast_to(own_edge, (LANES, ROWS))
-    kaug[FAR] = key_marks(jnp.logical_and(wide_there, image_rows(segs[FAR])))
-    in_crossing = jnp.broadcast_to(segs[OWN, 0:1, :], (LANES, ROWS)) == jnp.broadcast_to(own_edge, (LANES, ROWS))
-    helped[...] = jnp.where(jnp.logical_and(wide_there, in_crossing), 1.0, 0.0).T
-
-    expert_of = jnp.zeros((PACK, ROWS), jnp.int32)
-    place_iota = lax.broadcasted_iota(jnp.int32, (PACK, ROWS), 0)
-    for j, step in enumerate(STEPS):
-        expert_of = jnp.where(place_iota == j, moved(me, step, 1), expert_of)
-    chosen = jnp.broadcast_to(route_ref[0:1, :], (PACK, ROWS)) == expert_of
-    earlier = lax.broadcasted_iota(jnp.int32, (ROWS, ROWS), 0) < lax.broadcasted_iota(
-        jnp.int32, (ROWS, ROWS), 1
-    )
-    rank = jnp.dot(
-        jnp.where(chosen, 1.0, 0.0).astype(jnp.bfloat16),
-        jnp.where(earlier, 1.0, 0.0).astype(jnp.bfloat16),
-        preferred_element_type=jnp.float32,
-    )
-    slot = jnp.where(chosen, rank, -1.0)
-    slot_iota = lax.broadcasted_iota(jnp.int32, (CAP, ROWS), 0).astype(jnp.float32)
-    for j in range(PACK):
-        hit = jnp.broadcast_to(slot[j : j + 1, :], (CAP, ROWS)) == slot_iota
-        hit = jnp.where(hit, 1.0, 0.0)
-        place[CAP * j : CAP * (j + 1), :] = hit.astype(jnp.bfloat16)
-    for j in range(0, PACK * CAP, LANES):
-        place_t[:, j : j + LANES] = place[j : j + LANES, :].astype(jnp.float32).T.astype(jnp.bfloat16)
-    gate_cols[...] = jnp.broadcast_to(gate_ref[0:1, :], (LANES, ROWS)).T
-    stream[...] = res[...].astype(jnp.float32)
-
     exp_scale = float((1024 // HEADS) ** -0.5 * 1.4426950408889634)
     low_lanes = lax.broadcasted_iota(jnp.int32, (ROWS, LANES), 1) < LANES // 2
     ones = jnp.ones((ROWS, LANES), jnp.bfloat16)
@@ -225,15 +215,19 @@
         return (lambda: buf[at], lambda: kaug[place_of], lambda: buf[at + 1])
 
     def tiles_of(kind, p):
-        tiles = [at_home(p, OWN), at_home(p, SIB), arrived(near, 2 * p, NEAR)]
-        if kind == "home":
-            tiles.append(arrived(fwd, 2 * p, FWD))
-            if p < KEPT:
-                tiles.append(arrived(near, 2 * KEPT + 2 * p, FAR))
+        here = [at_home(p, OWN), at_home(p, SIB)]
+        if kind == "part":
+            return here
+        tiles = [arrived(near, 2 * p, NEAR)]
+        if kind == "help":
+            return here + tiles
+        tiles.append(arrived(fwd, 2 * p, FWD))
+        if p < KEPT:
+            tiles.append(arrived(near, 2 * KEPT + 2 * p, FAR))
         return tiles
 
     def begin_unit(kind, p, held, tops):
-        if kind == "home":
+        if kind != "help":
             both, marks = qs[:, p * LANES : (p + 1) * LANES], qaug[0]
         else:
             both, marks = near[2 * PAIRS + p - KEPT], qaug[1]
@@ -255,26 +249,32 @@
             )
             held[n] = scores
             top = scores if top is None else jnp.maximum(top, scores)
-        tops[...] = jnp.broadcast_to(jnp.max(top, axis=1, keepdims=True), (2 * ROWS, LANES))
+        top = jnp.broadcast_to(jnp.max(top, axis=1, keepdims=True), (2 * ROWS, LANES))
+        if kind == "home":
+            top = jnp.maximum(top, part_tops[p])
+        tops[...] = top
 
     def finish_unit(kind, p, held, tops):
         top = jnp.concatenate([tops[...], tops[...]], axis=1)
         summed = jnp.zeros((2 * ROWS, 2 * LANES), jnp.float32)
+        if kind == "home":
+            shrink = jnp.exp2((part_tops[p] - tops[...]) * exp_scale)
+            summed = parts[p] * jnp.concatenate([shrink, shrink], axis=1)
         for n, (_, _, value) in enumerate(tiles_of(kind, p)):
             weights = jnp.exp2((held[n] - top) * exp_scale).astype(jnp.bfloat16)
             rhs = jnp.concatenate([value(), ones], axis=1)
             summed = summed + jnp.dot(weights, rhs, preferred_element_type=jnp.float32)
+        if kind == "part":
+            parts[p] = summed
+            part_tops[p] = tops[...]
+            return
         both = summed[:, :LANES] / summed[:, LANES:]
         attended = jnp.where(low_lanes, both[:ROWS], both[ROWS:]).astype(jnp.bfloat16)
         if kind == "help":
             help_out[p - KEPT] = attended
             helping(p - KEPT).start()
-        elif p >= KEPT:
+        else:
             att[:, p * LANES : (p + 1) * LANES] = attended
-        else:
-            stream[...] += jnp.dot(
-                attended, wo[p * LANES : (p + 1) * LANES, :], preferred_element_type=jnp.float32
-            )
 
     came = set()
 
@@ -287,6 +287,8 @@
                 forward(at).start()
 
     def unit_came(kind, p):
+        if kind == "part":
+            return
         near_came(2 * p)
         near_came(2 * p + 1)
         if kind == "help":
@@ -295,15 +297,27 @@
             near_came(2 * KEPT + 2 * p)
             near_came(2 * KEPT + 2 * p + 1)
 
-    for at in range(4):
-        near_came(at)
+    def marks_of_two_hops():
+        for copy in seg_on:
+            copy.wait_recv()
+        kaug[FWD] = key_marks(image_rows(segs[FWD]))
+        far_edge = edge(segs[FAR, 0:1, :], core == 0)
+        wide_there = jnp.broadcast_to(far_edge, (LANES, ROWS)) == jnp.broadcast_to(own_edge, (LANES, ROWS))
+        kaug[FAR] = key_marks(jnp.logical_and(wide_there, image_rows(segs[FAR])))
+        in_crossing = jnp.broadcast_to(segs[OWN, 0:1, :], (LANES, ROWS)) == jnp.broadcast_to(own_edge, (LANES, ROWS))
+        helped[...] = jnp.where(jnp.logical_and(wide_there, in_crossing), 1.0, 0.0).T
+
     for copy in sib_out[2:]:
         copy.wait_recv()
-    loads[4].wait()
     stages = ((held_a, tops_a), (held_b, tops_b))
     for n, unit in enumerate(UNITS):
+        if n == 4:
+            for at in range(4):
+                near_came(at)
         for later in UNITS[n : n + 1 + AHEAD]:
             unit_came(*later)
+        if n == PAIRS:
+            marks_of_two_hops()
         if unit[0] == "home":
             forward(2 * unit[1]).wait_recv()
             forward(2 * unit[1] + 1).wait_recv()
@@ -312,6 +326,11 @@
             finish_unit(*UNITS[n - 1], *stages[(n - 1) % 2])
     finish_unit(*UNITS[-1], *stages[(len(UNITS) - 1) % 2])
 
+    loads[4].wait()
+    kept = KEPT * LANES
+    stream[...] = res[...].astype(jnp.float32) + jnp.dot(
+        att[:, :kept], wo[:kept, :], preferred_element_type=jnp.float32
+    )
     for n in range(PAIRS - KEPT):
         helping(n).wait_recv()
         c = slice((KEPT + n) * LANES, (KEPT + n + 1) * LANES)
@@ -426,10 +445,12 @@
             pltpu.VMEM((2 * KEPT, ROWS, LANES), bf16),
             pltpu.VMEM((PAIRS - KEPT, ROWS, LANES), bf16),
             pltpu.VMEM((PAIRS - KEPT, ROWS, LANES), bf16),
-            pltpu.VMEM((5, 2 * ROWS, ROWS), f32),
-            pltpu.VMEM((5, 2 * ROWS, ROWS), f32),
+            pltpu.VMEM((3, 2 * ROWS, ROWS), f32),
+            pltpu.VMEM((3, 2 * ROWS, ROWS), f32),
             pltpu.VMEM((2 * ROWS, LANES), f32),
             pltpu.VMEM((2 * ROWS, LANES), f32),
+            pltpu.VMEM((PAIRS, 2 * ROWS, 2 * LANES), f32),
+            pltpu.VMEM((PAIRS, 2 * ROWS, LANES), f32),
             pltpu.VMEM((5, 8, ROWS), jnp.int32),
             pltpu.VMEM((2, ROWS, LANES), bf16),
             pltpu.VMEM((5, ROWS, LANES), bf16),

time: 63.8 us -> 60.8 us (0.953)
  Pallas kernels: 61.8 us -> 58.8 us
    pallas_call x1, Pallas kernels: 61.8 us -> 58.8 us  [on_device(): pl.pallas_call(kernel, out_shape=jax.ShapeDtypeStruct((ROWS, 1024), bf16)...]
where the time goes in v4:
time: 60.8 us; the launch traced here: 60.6 us
  Pallas kernels  58.8 us (97%)
  local copies, waits for them, and re-layouts  1.87 us (3%)
    pallas_call x1, Pallas kernels, on_device(): pl.pallas_call(kernel, out_shape=jax.ShapeDtypeStruct((ROWS, 1024), bf16)...  58.8 us
    unnamed x1, local copies, waits for them, and re-layouts  1.87 us

profile of v4, /device:TPU:1, one launch (start us, length us, event | category | flops | bytes accessed | tf_op | source)
XLA Modules:
  0.0 60.6 jit_solution(6590558243854754272)
XLA Ops:
  0.0 58.8 %layer.1 = bf16[256,1024]{1,0:T(8,128)(2,1)} custom-call(bf16[256,1024]{1,0:T(8,128)(2,1)} %q_hbm.1, bf16[256,1024]{1,0:T(8,128)(2,1)} %k_hbm.1, bf16[256,1024]{1,0:T(8,128)(2,1)} %v_hbm.1, bf16[256,1024]{1,0:T(8,128)(2,1)} %res_hbm.1, s32[1,256]{1,0:T(1,128)} %bitcast.5, s32[1,256]{1,0:T(1,128)} %bitcast.6, f32[1,256]{1,0:T(1,128)} %bitcast.7, ...), custom_call_target="tpu_custom_call" | custom-call | tf_op jit(solution)/shard_map/layer/pallas_call | solution.py:434
  58.8 1.9 %copy.13 = bf16[256,1024]{1,0:T(8,128)(2,1)} copy(bf16[256,1024]{1,0:T(8,128)(2,1)} %layer.1) | data formatting | bytes 1048576

commit v5 on v4

--- a/solution.py
+++ b/solution.py
@@ -16,7 +16,7 @@
 MESH = pl.DeviceIdType.MESH
 OWN, SIB, NEAR, FAR, FWD = range(5)
 KEPT = 5
-WAVES = (0, 8, 20, 32)
+WAVES = (0, 8, 19, 27, 32)
 WIDE = 1024
 AHEAD = 1
 PICK_ORDER = (0, 1, 6, 2, 3, 7, 4, 5, 8, 9)
@@ -47,11 +47,11 @@
 
 def kernel(
     q_hbm, k_hbm, v_hbm, res_hbm, seg_ref, route_ref, gate_ref, gain_ref, wo_hbm, w1_hbm, w2_hbm,
-    out_ref,
+    out_hbm,
     qs, kt, vt, near, fwd, pick, help_out, help_in, held_a, held_b, tops_a, tops_b, parts, part_tops,
     segs, qaug, kaug, helped, att,
-    res, wo, w1, w2, stream, place, place_t, gate_cols, outg, recv, hid, prod, ret,
-    load_sem, seg_send, seg_recv, sib_send, sib_recv, near_send, near_recv, fwd_send, fwd_recv,
+    res, wo, w1, w2, stream, done, place, place_t, gate_cols, outg, recv, hid, prod, ret,
+    load_sem, out_sem, seg_send, seg_recv, sib_send, sib_recv, near_send, near_recv, fwd_send, fwd_recv,
     help_send, help_recv, go_send, go_recv, back_send, back_recv,
 ):
     me = lax.axis_index("pack")
@@ -397,8 +397,15 @@
     stream[...] += gate * jnp.dot(place_t[:, :ROWS], ret[:ROWS, :], preferred_element_type=jnp.float32)
     for j in range(HALF, PACK - 1):
         back[j].wait_recv()
-    second = jnp.dot(place_t[:, ROWS:], ret[ROWS:, :], preferred_element_type=jnp.float32)
-    out_ref[...] = (stream[...] + gate * second).astype(out_ref.dtype)
+    upper = ROWS // 2
+    leaving = []
+    for n in range(2):
+        r = slice(n * upper, (n + 1) * upper)
+        second = jnp.dot(place_t[r, ROWS:], ret[ROWS:, :], preferred_element_type=jnp.float32)
+        done[r, :] = (stream[r, :] + gate[r, :] * second).astype(done.dtype)
+        rows = pl.ds(n * upper, upper)
+        leaving.append(pltpu.make_async_copy(done.at[rows], out_hbm.at[rows], out_sem.at[n]))
+        leaving[n].start()
 
     for copy in seg_out + seg_on + sib_out:
         copy.wait_send()
@@ -420,6 +427,8 @@
         helping(n).wait_send()
     for copy in go + back:
         copy.wait_send()
+    for copy in leaving:
+        copy.wait()
 
 
 def on_device(
@@ -435,7 +444,7 @@
         kernel,
         out_shape=jax.ShapeDtypeStruct((ROWS, 1024), bf16),
         in_specs=[hbm] * 4 + [vmem] * 4 + [hbm] * 3,
-        out_specs=vmem,
+        out_specs=hbm,
         scratch_shapes=[
             pltpu.VMEM((ROWS, 1024), bf16),
             pltpu.VMEM((2, ROWS, 1024), bf16),
@@ -461,6 +470,7 @@
             pltpu.VMEM((1024, 2048), bf16),
             pltpu.VMEM((2048, 1024), bf16),
             pltpu.VMEM((ROWS, 1024), f32),
+            pltpu.VMEM((ROWS, 1024), bf16),
             pltpu.VMEM((PACK * CAP, ROWS), bf16),
             pltpu.VMEM((ROWS, PACK * CAP), bf16),
             pltpu.VMEM((ROWS, LANES), f32),
@@ -470,6 +480,7 @@
             pltpu.VMEM((PACK * CAP, 1024), bf16),
             pltpu.VMEM((PACK * CAP, 1024), bf16),
             dma((7,)),
+            dma((2,)),
             dma((4,)),
             dma((4,)),
             dma((2, 2)),

time: 60.8 us -> 59.9 us (0.985)
  Pallas kernels: 58.8 us -> 57.8 us
    pallas_call x1, Pallas kernels: 58.8 us -> 57.8 us  [on_device(): pl.pallas_call(kernel, out_shape=jax.ShapeDtypeStruct((ROWS, 1024), bf16)...]
where the time goes in v5:
time: 59.9 us; the launch traced here: 59.7 us
  Pallas kernels  57.8 us (96%)
  local copies, waits for them, and re-layouts  1.87 us (3%)
    pallas_call x1, Pallas kernels, on_device(): pl.pallas_call(kernel, out_shape=jax.ShapeDtypeStruct((ROWS, 1024), bf16)...  57.8 us
    unnamed x1, local copies, waits for them, and re-layouts  1.87 us

profile of v5, /device:TPU:1, one launch (start us, length us, event | category | flops | bytes accessed | tf_op | source)
XLA Modules:
  0.0 59.7 jit_solution(11927697728566274223)
XLA Ops:
  0.0 57.8 %layer.1 = bf16[256,1024]{1,0:T(8,128)(2,1)} custom-call(bf16[256,1024]{1,0:T(8,128)(2,1)} %q_hbm.1, bf16[256,1024]{1,0:T(8,128)(2,1)} %k_hbm.1, bf16[256,1024]{1,0:T(8,128)(2,1)} %v_hbm.1, bf16[256,1024]{1,0:T(8,128)(2,1)} %res_hbm.1, s32[1,256]{1,0:T(1,128)} %bitcast.5, s32[1,256]{1,0:T(1,128)} %bitcast.6, f32[1,256]{1,0:T(1,128)} %bitcast.7, ...), custom_call_target="tpu_custom_call" | custom-call | tf_op jit(solution)/shard_map/layer/pallas_call | solution.py:443
  57.8 1.9 %copy.13 = bf16[256,1024]{1,0:T(8,128)(2,1)} copy(bf16[256,1024]{1,0:T(8,128)(2,1)} %layer.1) | data formatting | bytes 1048576
